TPU v7x, 512 devices: a whole 4x4x16 slice. The times are simulated.
512 devices in a mesh: seq: 32 (over x, z_lo), exp: 16 (over z_hi, y, core).
Axes of the slice: x: 4, y: 4, z: 16 (z_hi: 2, z_lo: 8; z = z_hi * 8 + z_lo), core: 2. Of those that a mesh axis runs over, the one named last changes fastest.
Arguments:
- tokens: bfloat16 [8, 8192, 2048], P(None, 'seq', 'exp'), may hold values from -6 to 6
- grad_out: bfloat16 [8, 8192, 2048], P(None, 'seq', 'exp'), may hold values from -6 to 6
- logits: float32 [8, 16, 8192], P(None, None, 'seq'), may hold values from -12 to 312
- slot_params: bfloat16 [16, 2048], P(None, 'exp'), may hold values from -6 to 6
- weight_in: bfloat16 [16, 2048, 4096], P('exp', None, 'seq'), may hold values from -0.125 to 0.125
- weight_out: bfloat16 [16, 4096, 2048], P('exp', 'seq'), may hold values from -0.09375 to 0.09375
Outputs:
- grad_tokens: bfloat16 [8, 8192, 2048], P(None, 'seq', 'exp')
- grad_slots: float32 [16, 2048], P(None, 'exp')
- grad_weight_in: bfloat16 [16, 2048, 4096], P('exp', None, 'seq')
- grad_weight_out: bfloat16 [16, 4096, 2048], P('exp', 'seq')
All inputs are finite; a program needn't handle non-finite values.
Results may differ from a plain program's by a relative error of at most 0.024.
Values may be sent and summed in bfloat16 or wider, within the bound.
A program may use at most 64 MiB of HBM per device.

v0:
```python
import jax
import jax.numpy as jnp
from jax import lax
from jax.sharding import PartitionSpec as P

root_coef = 0.7978845608028654
cubic_coef = 0.044715


def merged(value, axis, join):
    pieces = jax.tree.map(lambda part: lax.all_gather(part, axis), value)
    head = jax.tree.map(lambda part: part[0], pieces)
    tail = jax.tree.map(lambda part: part[1:], pieces)
    running, _ = lax.scan(lambda running, piece: (join(running, piece), None), head, tail)
    return running


def gelu_parts(pre_act):
    tanh_value = jnp.tanh(root_coef * (pre_act + cubic_coef * pre_act * pre_act * pre_act))
    activated = 0.5 * pre_act * (1.0 + tanh_value)
    derivative = 0.5 * (1.0 + tanh_value) + 0.5 * pre_act * (
        1.0 - tanh_value * tanh_value
    ) * root_coef * (1.0 + 3.0 * cubic_coef * pre_act * pre_act)
    return (activated, derivative)


def merge_softmax(left_pair, right_pair):
    top_left, sum_left = left_pair
    top_right, sum_right = right_pair
    top_both = jnp.maximum(top_left, top_right)
    return (
        top_both,
        sum_left * jnp.exp(top_left - top_both) + sum_right * jnp.exp(top_right - top_both),
    )


def body(tokens, grad_out, logits, slot_params, weight_in, weight_out):
    top_local = jnp.max(logits, axis=2)
    sum_local = jnp.sum(jnp.exp(logits - top_local[:, :, None]), axis=2)
    top_logit, total_mass = merged((top_local, sum_local), "seq", merge_softmax)
    dispatch = jnp.exp(logits - top_logit[:, :, None]) / total_mass[:, :, None]
    combine = jax.nn.softmax(logits, axis=1)
    slot_part = jnp.einsum(
        "csm,cmd->csd", dispatch.astype(jnp.bfloat16), tokens, preferred_element_type=jnp.float32
    )
    grad_part = jnp.einsum(
        "csm,cmd->csd", combine.astype(jnp.bfloat16), grad_out, preferred_element_type=jnp.float32
    )
    slot_in, slot_grad = lax.psum((slot_part, grad_part), "seq")
    rows_in, rows_grad = (
        lax.all_to_all(
            slot_in.astype(jnp.bfloat16), "exp", split_axis=1, concat_axis=2, tiled=True
        ),
        lax.all_to_all(
            slot_grad.astype(jnp.bfloat16), "exp", split_axis=1, concat_axis=2, tiled=True
        ),
    )
    pre_act = jnp.einsum("ced,edf->cef", rows_in, weight_in, preferred_element_type=jnp.float32)
    activated, derivative = gelu_parts(pre_act)
    act_b = activated.astype(jnp.bfloat16)
    out_part = jnp.einsum("cef,efd->ced", act_b, weight_out, preferred_element_type=jnp.float32)
    act_grad = jnp.einsum("ced,efd->cef", rows_grad, weight_out, preferred_element_type=jnp.float32)
    pre_grad = (act_grad * derivative).astype(jnp.bfloat16)
    grad_weight_out = jnp.einsum(
        "cef,ced->efd", act_b, rows_grad, preferred_element_type=jnp.float32
    ).astype(jnp.bfloat16)
    grad_weight_in = jnp.einsum(
        "ced,cef->edf", rows_in, pre_grad, preferred_element_type=jnp.float32
    ).astype(jnp.bfloat16)
    back_part = jnp.einsum("cef,edf->ced", pre_grad, weight_in, preferred_element_type=jnp.float32)
    out_pieces, back_pieces = (
        lax.all_to_all(out_part, "exp", split_axis=2, concat_axis=1, tiled=True),
        lax.all_to_all(back_part, "exp", split_axis=2, concat_axis=1, tiled=True),
    )
    slot_out, slot_back = lax.psum((out_pieces, back_pieces), "seq")
    back_b = slot_back.astype(jnp.bfloat16)
    stat_part = jnp.sum(back_b.astype(jnp.float32) * slot_in, axis=2)
    out_b = slot_out.astype(jnp.bfloat16)
    comb_part = jnp.einsum("csd,cmd->csm", out_b, grad_out, preferred_element_type=jnp.float32)
    disp_part = jnp.einsum("csd,cmd->csm", back_b, tokens, preferred_element_type=jnp.float32)
    comb_grad, disp_grad, disp_stat = lax.psum((comb_part, disp_part, stat_part), "exp")
    logit_grad = combine * (
        comb_grad - jnp.sum(combine * comb_grad, axis=1, keepdims=True)
    ) + dispatch * (disp_grad - disp_stat[:, :, None])
    token_grad = jnp.einsum(
        "csm,csd->cmd", dispatch, slot_back, precision=lax.Precision.HIGHEST
    ) + jnp.einsum(
        "csm,sd->cmd", logit_grad, slot_params.astype(jnp.float32), precision=lax.Precision.HIGHEST
    )
    slot_term = jnp.einsum(
        "csm,cmd->sd", logit_grad.astype(jnp.bfloat16), tokens, preferred_element_type=jnp.float32
    )
    grad_slots = lax.psum(slot_term, "seq")
    return (token_grad.astype(jnp.bfloat16), grad_slots, grad_weight_in, grad_weight_out)


def solution(mesh):
    in_specs = (
        P(None, "seq", "exp"),
        P(None, "seq", "exp"),
        P(None, None, "seq"),
        P(None, "exp"),
        P("exp", None, "seq"),
        P("exp", "seq", None),
    )
    out_specs = (
        P(None, "seq", "exp"),
        P(None, "exp"),
        P("exp", None, "seq"),
        P("exp", "seq", None),
    )
    return jax.shard_map(body, mesh=mesh, in_specs=in_specs, out_specs=out_specs, check_vma=False)
```

profile of v0, /device:TPU:1, one launch (start us, length us, event | category | flops | bytes accessed | tf_op | source)
XLA Modules:
  0.0 1767.6 jit_solution(10605014074340372304)
XLA Ops:
  7.2 0.0 copy-start
  7.2 0.0 copy-start.1
  7.2 0.0 all-reduce.7.cloned.1.call-start
  7.2 1.1 reduce_max.18
  8.3 0.0 copy-done.1
  8.3 0.2 exponential_reduce_fusion
  8.5 112.3 %all-gather = f32[256,16]{1,0:T(8,128)S(1)} all-gather(f32[8,16]{1,0:T(8,128)S(1)} %reduce_max.18), channel_id=2, replica_groups=mesh['seq'=32,'exp'=16] {'seq'}, dimensions={0}, use_global_device_ids=true | all-gather | bytes 16896 | tf_op jit(solution)/shard_map/all_gather | solution.py:11
  120.8 98.3 %all-gather.1 = f32[256,16]{1,0:T(8,128)S(1)} all-gather(f32[8,16]{1,0:T(8,128)S(1)} %exponential_reduce_fusion), channel_id=3, replica_groups=mesh['seq'=32,'exp'=16] {'seq'}, dimensions={0}, use_global_device_ids=true | all-gather | bytes 16896 | tf_op jit(solution)/shard_map/all_gather | solution.py:11
  219.1 0.6 copy-done.8
  219.8 0.0 slice-start
  219.8 0.7 slice-done
  220.4 1.1 while.12
  221.6 0.0 copy-start.3
  221.6 0.9 fusion.18
  222.4 0.0 all-reduce.7.cloned.1.call-update
  222.5 425.3 %all-reduce.7.cloned.1.call-done = f32[8,16,128]{2,1,0:T(8,128)} async-done(((f32[8,16,128]{2,1,0:T(8,128)}), f32[8,16,128]{2,1,0:T(8,128)}) %all-reduce.7.cloned.1.call-update) | async-done | bytes 65552 | tf_op jit(solution)/shard_map/psum | solution.py:49
  647.8 0.8 convert_element_type.49
  648.6 40.1 %all_to_all.42 = bf16[8,16,128]{2,0,1:T(8,128)(2,1)S(1)} all-to-all(bf16[8,16,128]{2,0,1:T(8,128)(2,1)S(1)} %copy.12), channel_id=1, replica_groups=mesh['seq'=32,'exp'=16] {'exp'}, dimensions={1} | all-to-all | bytes 65536 | tf_op jit(solution)/shard_map/all_to_all | solution.py:51
  688.7 0.2 convolution_bitcast_fusion.1
  688.9 0.4 fusion.14
  689.3 0.5 broadcast.43
  689.8 9.3 reduce
  699.1 0.0 copy-start.6
  699.2 1.2 reshape.81
  700.3 3.7 all-to-all-start.3
  704.0 0.6 fusion.39
  704.6 0.0 copy-done.6
  704.6 0.2 fusion.20
  704.8 13.8 all-to-all-done.3
  718.6 0.8 reduce.1
  719.4 1.6 reshape.82
  721.1 0.3 copy.18
  721.4 197.4 %all-reduce.12 = (bf16[8,16,128]{2,1,0:T(8,128)(2,1)S(1)}, bf16[8,16,128]{2,1,0:T(8,128)(2,1)S(1)}) all-reduce(f32[8,16,128]{2,1,0:T(8,128)S(1)} %fusion.20, f32[8,16,128]{2,1,0:T(8,128)S(1)} %copy.18), channel_id=1, replica_groups=mesh['seq'=32,'exp'=16] {'seq'}, use_global_device_ids=true, to_apply=%region_6.7 | all-reduce | flops 32768 | bytes 196608 | tf_op jit(solution)/shard_map/psum | solution.py:49
  918.7 45.3 %all_to_all.43 = bf16[8,16,128]{2,0,1:T(8,128)(2,1)S(1)} all-to-all(bf16[8,16,128]{2,0,1:T(8,128)(2,1)S(1)} %copy.11), channel_id=1, replica_groups=mesh['seq'=32,'exp'=16] {'exp'}, dimensions={1} | all-to-all | bytes 65536 | tf_op jit(solution)/shard_map/all_to_all | solution.py:54
  964.0 0.2 fusion.10
  964.3 0.3 fusion.11
  964.5 9.3 reduce.2
  973.9 0.0 copy-start.7
  973.9 1.2 reshape.79
  975.1 3.7 all-to-all-start.2
  978.8 0.0 all-reduce.9.cloned.1.call-start
  978.8 0.9 fusion.40
  979.7 1.1 fusion.4
  980.8 12.5 all-to-all-done.2
  993.4 0.8 reduce.3
  994.2 1.6 reshape.80
  995.8 0.9 copy.17
  996.8 0.0 all-reduce.9.cloned.1.call-update
  996.8 0.0 all-reduce.11.cloned.1.call-start
  996.8 1.2 fusion.3
  998.0 387.8 %all-reduce.9.cloned.1.call-done = f32[8,16,128]{2,1,0:T(8,128)} async-done(((f32[8,16,128]{2,1,0:T(8,128)}), f32[8,16,128]{2,1,0:T(8,128)}) %all-reduce.9.cloned.1.call-update) | async-done | bytes 65552 | tf_op jit(solution)/shard_map/psum | solution.py:75
  1385.8 1.7 fusion.28
  1387.6 0.0 all-reduce.11.cloned.1.call-update
  1387.6 0.8 copy-done.5
  1388.4 0.0 copy-done.10
  1388.5 0.1 multiply_reduce_fusion.1
  1388.6 73.5 %psum.62 = f32[8,16]{1,0:T(8,128)S(1)} all-reduce(f32[8,16]{1,0:T(8,128)S(1)} %multiply_reduce_fusion.1), channel_id=1, replica_groups=mesh['seq'=32,'exp'=16] {'exp'}, use_global_device_ids=true, to_apply=%region_14.15 | all-reduce | flops 128 | bytes 1024 | tf_op jit(solution)/shard_map/psum | solution.py:81
  1462.1 2.0 fusion.38
  1464.1 189.5 %all-reduce.11.cloned.1.call-done = (f32[8,16,256]{2,1,0:T(8,128)}, f32[8,16,256]{2,1,0:T(8,128)}) async-done(((f32[8,16,256]{2,1,0:T(8,128)}, f32[8,16,256]{2,1,0:T(8,128)}), (f32[8,16,256]{2,1,0:T(8,128)}, f32[8,16,256]{2,1,0:T(8,128)})) %all-reduce.11.cloned.1.call-update) | async-done | bytes 262160 | tf_op jit(solution)/shard_map/psum | solution.py:81
  1653.6 1.0 multiply_reduce_fusion
  1654.6 0.1 multiply_add_fusion
  1654.8 0.2 convolution_bitcast_fusion
  1654.9 104.3 %psum.63 = f32[16,128]{1,0:T(8,128)} all-reduce(f32[16,128]{1,0:T(8,128)S(1)} %convolution_bitcast_fusion), channel_id=1, replica_groups=mesh['seq'=32,'exp'=16] {'seq'}, use_global_device_ids=true, to_apply=%region_15.16 | all-reduce | flops 2048 | bytes 16384 | tf_op jit(solution)/shard_map/psum | solution.py:93
  1759.2 1.8 fusion.5
  (52 shorter events, 0.6 us)
Async XLA Ops:
  7.2 214.4 %copy-start = (bf16[8,256,128]{2,1,0:T(8,128)(2,1)S(1)}, bf16[8,256,128]{2,1,0:T(8,128)(2,1)}, u32[]{:S(2)}) copy-start(bf16[8,256,128]{2,1,0:T(8,128)(2,1)} %param.8) | copy-start | bytes 1572868
  7.2 1.1 copy-start.1
  7.2 640.6 %all-reduce.7.cloned.1.call-start = ((), (), s32[]{:S(2)}) async-start(), calls=%async_computation.4 | async-start | bytes 131072 | tf_op jit(solution)/shard_map/psum | solution.py:49
  219.1 0.7 copy-start.8
  219.8 0.7 slice-start
  221.6 467.2 %copy-start.3 = (bf16[1,2048,128]{2,1,0:T(8,128)(2,1)S(1)}, bf16[1,2048,128]{2,1,0:T(8,128)(2,1)}, u32[]{:S(2)}) copy-start(bf16[1,2048,128]{2,1,0:T(8,128)(2,1)} %param.12) | copy-start | bytes 1572868
  222.4 466.5 %copy-start.2 = (bf16[1,128,2048]{2,1,0:T(8,128)(2,1)S(1)}, bf16[1,128,2048]{2,1,0:T(8,128)(2,1)}, u32[]{:S(2)}) copy-start(bf16[1,128,2048]{2,1,0:T(8,128)(2,1)} %param.13) | copy-start | bytes 1572868
  699.1 5.5 copy-start.6
  700.3 18.3 %all-to-all-start.3 = ((f32[16,1,1024]{2,1,0:T(1,128)}), f32[16,1,1024]{2,1,0:T(1,128)S(1)}, u32[]{:S(2)}, u32[]{:S(2)}) async-start(f32[16,1,1024]{2,1,0:T(1,128)} %reshape.81), calls=%async_computation.3 | async-start | bytes 131072 | tf_op jit(solution)/shard_map/all_to_all | solution.py:72
  721.4 242.9 %copy-start.4 = (bf16[1,2048,128]{2,1,0:T(8,128)(2,1)S(1)}, bf16[1,2048,128]{2,1,0:T(8,128)(2,1)}, u32[]{:S(2)}) copy-start(bf16[1,2048,128]{2,1,0:T(8,128)(2,1)} %param.12) | copy-start | bytes 1572868
  973.9 4.9 copy-start.7
  975.1 18.3 %all-to-all-start.2 = ((f32[16,1,1024]{2,1,0:T(1,128)}), f32[16,1,1024]{2,1,0:T(1,128)S(1)}, u32[]{:S(2)}, u32[]{:S(2)}) async-start(f32[16,1,1024]{2,1,0:T(1,128)} %reshape.79), calls=%async_computation.2 | async-start | bytes 131072 | tf_op jit(solution)/shard_map/all_to_all | solution.py:73
  978.8 407.1 %all-reduce.9.cloned.1.call-start = ((), (), s32[]{:S(2)}) async-start(), calls=%async_computation.5 | async-start | bytes 131072 | tf_op jit(solution)/shard_map/psum | solution.py:75
  996.8 656.8 %all-reduce.11.cloned.1.call-start = ((), (), s32[]{:S(2)}) async-start(), calls=%async_computation.6 | async-start | bytes 524288 | tf_op jit(solution)/shard_map/psum | solution.py:81
  1387.6 0.8 copy-start.5
  1387.6 0.9 copy-start.10
  1653.6 1.0 copy-start.9
  1653.6 1.0 copy-start.11
  1654.9 104.3 %copy-start.12 = (bf16[16,128]{1,0:T(8,128)(2,1)S(1)}, bf16[16,128]{1,0:T(8,128)(2,1)}, u32[]{:S(2)}) copy-start(bf16[16,128]{1,0:T(8,128)(2,1)} %param.11) | copy-start | bytes 12292
Sparse Core Ops, SparseCore 0:
  222.6 425.1 all-reduce.6
  996.9 388.8 all-reduce.8
  1389.4 264.1 all-reduce.10
where the time goes:
time: 1780 us; the launch traced here: 1770 us
  waiting for transfers between devices  1030 us (58%)
  blocking collectives  671 us (38%)
  other arithmetic  24.7 us (1%)
    psum x1, waiting for transfers between devices, body(): slot_in, slot_grad = lax.psum((slot_part, grad_part), 'seq')  425 us
    psum x1, waiting for transfers between devices, body(): slot_out, slot_back = lax.psum((out_pieces, back_pieces), 'seq')  388 us
    all_gather x2, blocking collectives, merged(): pieces = jax.tree.map(lambda part: lax.all_gather(part, axis), value)  211 us
    psum x1, blocking collectives, body(): slot_in, slot_grad = lax.psum((slot_part, grad_part), 'seq')  197 us
    psum x1, waiting for transfers between devices, body(): lax.psum((comb_part, disp_part, stat_part), 'exp')  190 us
    psum x1, blocking collectives, body(): grad_slots = lax.psum(slot_term, 'seq')  104 us
    psum x1, blocking collectives, body(): lax.psum((comb_part, disp_part, stat_part), 'exp')  73.5 us
    all_to_all x1, blocking collectives, body(): lax.all_to_all(slot_grad.astype(jnp.bfloat16), 'exp', split_axis=1, conca...  45.3 us
  transfers between devices with their start and end apart: 5, of which 5 were waited for; matrix products, arithmetic and copies ran while one was open for 0% of the time, Pallas kernels for 0%

commit v1 on v0

v1 whole, which is shorter than its diff:
```python
import functools

import jax
import jax.numpy as jnp
from jax import lax
from jax.experimental import pallas as pl
from jax.experimental.pallas import tpu as pltpu
from jax.sharding import PartitionSpec as P

root_coef = 0.7978845608028654
cubic_coef = 0.044715
MESH = pl.DeviceIdType.MESH
f32 = jnp.float32
bf16 = jnp.bfloat16
LINE = 8


def gelu_parts(pre_act):
    tanh_value = jnp.tanh(root_coef * (pre_act + cubic_coef * pre_act * pre_act * pre_act))
    activated = 0.5 * pre_act * (1.0 + tanh_value)
    derivative = 0.5 * (1.0 + tanh_value) + 0.5 * pre_act * (
        1.0 - tanh_value * tanh_value
    ) * root_coef * (1.0 + 3.0 * cubic_coef * pre_act * pre_act)
    return (activated, derivative)


def dot(a, b, ca, cb):
    return lax.dot_general(a, b, (((ca,), (cb,)), ((), ())), preferred_element_type=f32)


def wait_for(ref, sem):
    pltpu.make_async_copy(ref, ref, sem).wait()


def each(count, step):
    def run(i, carry):
        step(i)
        return carry

    lax.fori_loop(0, count, run, 0)


def kernel(
    S, E, C,
    tokens_h, grad_h, logits_h, params_h, win_h, wout_h,
    gtok_h, gslot_h, gwin_h, gwout_h,
    tokens, grad, logits, params, win, wout,
    gtok, gslot, gwin, gwout,
    comb, disp,
    send1, recv1, send2, rows, send3, recv3, send4, recv4,
    send5, recv5, send6, recv6, recv7, recv8,
    slot_keep, lse_keep,
    in_sem, out_sem, send_sem, recv_sem,
):
    s = lax.axis_index("seq")
    x = lax.axis_index("exp")
    half = LINE // 2
    Q = E // 2
    per = C // Q
    q = lax.rem(x, Q)
    side = x - q
    across = lax.rem(x + Q, E)

    def owner(e):
        return lax.div(e, half) * LINE + LINE // 4 + lax.rem(e, half)

    z = lax.rem(s, LINE)
    is_owner = jnp.logical_and(z >= LINE // 4, z < LINE // 4 + half)
    mine = lax.div(s, LINE) * half + jnp.clip(z - LINE // 4, 0, half - 1)
    both = jnp.logical_and(is_owner, mine == x)
    home = owner(x)

    loads = []
    for i, (a, b) in enumerate(
        ((logits_h, logits), (tokens_h, tokens), (grad_h, grad), (win_h, win), (wout_h, wout), (params_h, params))
    ):
        copy = pltpu.make_async_copy(a, b, in_sem.at[i])
        copy.start()
        loads.append(copy)

    barrier = pltpu.get_barrier_semaphore()

    def greet(ds, dx):
        pl.semaphore_signal(barrier, inc=1, device_id=(ds, dx), device_id_type=MESH)

    each(S - 1, lambda i: greet(lax.rem(s + 1 + i, S), x))
    each(Q - 1, lambda i: greet(s, side + lax.rem(q + 1 + i, Q)))
    greet(s, across)
    each(E - 1, lambda i: greet(home, lax.rem(x + 1 + i, E)))

    @pl.when(jnp.logical_not(both))
    def _():
        greet(home, x)

    @pl.when(is_owner)
    def _():
        each(S - 1, lambda i: greet(lax.rem(s + 1 + i, S), mine))

        @pl.when(jnp.logical_not(both))
        def _():
            greet(s, mine)

    def send(src, dst, k, ds, dx):
        pltpu.make_async_remote_copy(
            src_ref=src, dst_ref=dst, send_sem=send_sem.at[k], recv_sem=recv_sem.at[k],
            device_id=(ds, dx), device_id_type=MESH,
        ).start()

    def keep(src, dst, k):
        pltpu.make_async_copy(src, dst, recv_sem.at[k]).start()

    def sent(ref, k):
        wait_for(ref, send_sem.at[k])

    loads[0].wait()
    loads[1].wait()
    loads[2].wait()
    slot_parts, grad_parts, lse_parts = [], [], []
    for c in range(C):
        value = logits[c]
        top = jnp.max(value, axis=1, keepdims=True)
        weight = jnp.exp(value - top)
        mass = jnp.sum(weight, axis=1, keepdims=True)
        slot_parts.append(dot((weight / mass).astype(bf16), tokens[c], 1, 0))
        lse_parts.append(jnp.broadcast_to(top + jnp.log(mass), (E, 128)))
        crest = jnp.max(value, axis=0, keepdims=True)
        share = jnp.exp(value - crest)
        share = share / jnp.sum(share, axis=0, keepdims=True)
        comb[c] = share
        grad_parts.append(dot(share.astype(bf16), grad[c], 1, 0))
    send1[:, 0:8, :] = jnp.swapaxes(jnp.stack(slot_parts), 0, 1)
    send1[:, 8:16, :] = jnp.swapaxes(jnp.stack(grad_parts), 0, 1)
    send1[:, 16:24, :] = jnp.swapaxes(jnp.stack(lse_parts), 0, 1)

    flag = is_owner.astype(jnp.int32)
    pl.semaphore_wait(barrier, S - 1 + Q - 1 + 1 + E + flag * S - 2 * both.astype(jnp.int32))

    def to_owner(i):
        e = lax.rem(x + s + i, E)
        to = owner(e)

        @pl.when(to != s)
        def _():
            send(send1.at[e], recv1.at[s], 0, to, x)

        @pl.when(to == s)
        def _():
            keep(send1.at[e], recv1.at[s], 0)

    each(E, to_owner)

    @pl.when(is_owner)
    def _():
        wait_for(recv1, recv_sem.at[0])
        top = lax.fori_loop(1, S, lambda i, t: jnp.maximum(t, recv1[i, 16:24, :]), recv1[0, 16:24, :])

        def add(i, carry):
            total, slots, grads = carry
            weight = jnp.exp(recv1[i, 16:24, :] - top)
            return total + weight, slots + weight * recv1[i, 0:8, :], grads + recv1[i, 8:16, :]

        zero = jnp.zeros((8, 128), f32)
        total, slots, grads = lax.fori_loop(0, S, add, (zero, zero, zero))
        slots = slots / total
        slot_keep[...] = slots
        lse_keep[...] = top + jnp.log(total)
        send2[...] = jnp.concatenate([slots, grads], axis=0).astype(bf16)

        each(S - 1, lambda i: send(send2, rows.at[x], 1, lax.rem(s + 1 + i, S), mine))

        @pl.when(jnp.logical_not(both))
        def _():
            send(send2, rows.at[x], 1, s, mine)

        @pl.when(both)
        def _():
            keep(send2, rows.at[x], 1)

    loads[3].wait()
    loads[4].wait()
    wait_for(rows, recv_sem.at[1])
    held = jnp.concatenate([rows[i] for i in range(E)], axis=1)
    pre_act = dot(held, win[...], 1, 0)
    act_grad = dot(held, wout[...], 1, 1)
    activated, derivative = gelu_parts(pre_act[0:8])
    pre_grad = act_grad[8:16] * derivative
    stacked = jnp.concatenate([activated, pre_grad], axis=0).astype(bf16)
    out_part = dot(stacked, wout[...], 1, 0)
    back_part = dot(stacked, win[...], 1, 1)
    for i in range(E):
        cut = slice(i * 128, i * 128 + 128)
        send3[i] = jnp.concatenate([out_part[0:8, cut], back_part[8:16, cut]], axis=0).astype(bf16)

    def to_home(i):
        to = lax.rem(x + s + i, E)
        own = jnp.logical_and(both, to == x)

        @pl.when(jnp.logical_not(own))
        def _():
            send(send3.at[to], recv3.at[s], 2, home, to)

        @pl.when(own)
        def _():
            keep(send3.at[to], recv3.at[s], 2)

    each(E, to_home)

    blank = jnp.zeros((8, 128), f32)
    gwout[...] = dot(jnp.concatenate([blank, activated], axis=0).astype(bf16), held, 0, 0).astype(bf16)
    gwin[...] = dot(held, jnp.concatenate([pre_grad, blank], axis=0).astype(bf16), 0, 0).astype(bf16)
    store_out = pltpu.make_async_copy(gwout, gwout_h, out_sem.at[0])
    store_in = pltpu.make_async_copy(gwin, gwin_h, out_sem.at[1])
    store_out.start()
    store_in.start()

    @pl.when(is_owner)
    def _():
        wait_for(recv3, recv_sem.at[2])
        total = lax.fori_loop(0, S, lambda i, t: t + recv3[i].astype(f32), jnp.zeros((16, 128), f32))
        send4[0:16, :] = total
        stat = jnp.sum(total[8:16].astype(bf16).astype(f32) * slot_keep[...], axis=1, keepdims=True)
        lane = lax.broadcasted_iota(jnp.int32, (8, 128), 1)
        send4[16:24, :] = jnp.where(lane < 64, lse_keep[...], stat)
        each(S - 1, lambda i: send(send4, recv4.at[mine], 3, lax.rem(s + 1 + i, S), x))
        keep(send4, recv4.at[mine], 3)

    wait_for(recv4, recv_sem.at[3])
    outs = jnp.swapaxes(recv4[:, 0:8, :], 0, 1)
    backs = jnp.swapaxes(recv4[:, 8:16, :], 0, 1)
    stats = jnp.swapaxes(recv4[:, 16:24, :], 0, 1)
    for c in range(C):
        comb_grad = dot(outs[c].astype(bf16), grad[c], 1, 1)
        disp_grad = dot(backs[c].astype(bf16), tokens[c], 1, 1)
        dispatch = jnp.exp(logits[c] - stats[c][:, 0:1])
        share = comb[c]
        disp[c] = dispatch
        send5[c] = share * (
            comb_grad - jnp.sum(share * comb_grad, axis=0, keepdims=True)
        ) + dispatch * (disp_grad - stats[c][:, 64:65])

    def to_peer(i):
        to = lax.rem(q + 1 + i, Q)
        send(send5.at[pl.ds(to * per, per)], recv5.at[q], 4, s, side + to)

    each(Q - 1, to_peer)
    keep(send5.at[pl.ds(q * per, per)], recv5.at[q], 4)
    wait_for(recv5, recv_sem.at[4])
    part = recv5[0]
    for i in range(1, Q):
        part = part + recv5[i]
    send6[...] = part
    send(send6, recv6, 5, s, across)
    wait_for(recv6, recv_sem.at[5])
    recv7[q] = (send6[...] + recv6[...]).astype(bf16)
    each(Q - 1, lambda i: send(recv7.at[q], recv7.at[q], 6, s, side + lax.rem(q + 1 + i, Q)))
    loads[5].wait()
    wait_for(recv7.at[pl.ds(0, Q - 1)], recv_sem.at[6])

    term = jnp.zeros((E, 128), f32)
    for c in range(C):
        term = term + dot(recv7[c // per, c % per], tokens[c], 1, 0)
    recv8[s] = term.astype(bf16)
    each(S - 1, lambda i: send(recv8.at[s], recv8.at[s], 7, lax.rem(s + 1 + i, S), x))

    for c in range(C):
        left = jnp.concatenate([disp[c].astype(bf16), recv7[c // per, c % per]], axis=0)
        right = jnp.concatenate([backs[c].astype(bf16), params[...]], axis=0)
        gtok[c] = dot(left, right, 0, 0).astype(bf16)
    store_tok = pltpu.make_async_copy(gtok, gtok_h, out_sem.at[2])
    store_tok.start()

    wait_for(recv8.at[pl.ds(0, S - 1)], recv_sem.at[7])
    total = recv8[0].astype(f32)
    for i in range(1, S):
        total = total + recv8[i].astype(f32)
    gslot[...] = total
    store_slot = pltpu.make_async_copy(gslot, gslot_h, out_sem.at[3])
    store_slot.start()

    sent(send1.at[pl.ds(0, E - 1)], 0)

    @pl.when(jnp.logical_not(is_owner))
    def _():
        sent(send1.at[0], 0)

    @pl.when(is_owner)
    def _():
        each(S - 1, lambda i: sent(send2, 1))

        @pl.when(jnp.logical_not(both))
        def _():
            sent(send2, 1)

        each(S - 1, lambda i: sent(send4, 3))

    sent(send3.at[pl.ds(0, E - 1)], 2)

    @pl.when(jnp.logical_not(both))
    def _():
        sent(send3.at[0], 2)

    sent(recv5.at[pl.ds(0, Q - 1)], 4)
    sent(send6, 5)
    sent(recv7.at[pl.ds(0, Q - 1)], 6)
    sent(recv8.at[pl.ds(0, S - 1)], 7)
    store_out.wait()
    store_in.wait()
    store_tok.wait()
    store_slot.wait()


def solution(mesh):
    S, E = mesh.shape["seq"], mesh.shape["exp"]

    def body(tokens, grad_out, logits, slot_params, weight_in, weight_out):
        C, M, D = tokens.shape
        _, wide, F = weight_in.shape
        args = (tokens, grad_out, logits, slot_params, weight_in[0], weight_out[0])
        outs = (
            jax.ShapeDtypeStruct((C, M, D), bf16),
            jax.ShapeDtypeStruct((E, D), f32),
            jax.ShapeDtypeStruct((wide, F), bf16),
            jax.ShapeDtypeStruct((F, wide), bf16),
        )
        Q = E // 2
        per = C // Q
        hold = lambda a: pltpu.VMEM(a.shape, a.dtype)
        scratch = (
            [hold(a) for a in args]
            + [hold(a) for a in outs]
            + [
                pltpu.VMEM((C, E, M), f32),
                pltpu.VMEM((C, E, M), f32),
                pltpu.VMEM((E, 24, D), f32),
                pltpu.VMEM((S, 24, D), f32),
                pltpu.VMEM((16, D), bf16),
                pltpu.VMEM((E, 16, D), bf16),
                pltpu.VMEM((E, 16, D), bf16),
                pltpu.VMEM((S, 16, D), bf16),
                pltpu.VMEM((24, D), f32),
                pltpu.VMEM((E, 24, D), f32),
                pltpu.VMEM((C, E, M), f32),
                pltpu.VMEM((Q, per, E, M), f32),
                pltpu.VMEM((per, E, M), f32),
                pltpu.VMEM((per, E, M), f32),
                pltpu.VMEM((Q, per, E, M), bf16),
                pltpu.VMEM((S, E, D), bf16),
                pltpu.VMEM((8, D), f32),
                pltpu.VMEM((8, D), f32),
                pltpu.SemaphoreType.DMA((6,)),
                pltpu.SemaphoreType.DMA((4,)),
                pltpu.SemaphoreType.DMA((8,)),
                pltpu.SemaphoreType.DMA((8,)),
            ]
        )
        gtok, gslot, gwin, gwout = pl.pallas_call(
            functools.partial(kernel, S, E, C),
            out_shape=outs,
            in_specs=[pl.BlockSpec(memory_space=pl.ANY)] * 6,
            out_specs=[pl.BlockSpec(memory_space=pl.ANY)] * 4,
            scratch_shapes=scratch,
            compiler_params=pltpu.CompilerParams(
                collective_id=0, has_side_effects=True, vmem_limit_bytes=48 << 20
            ),
            name="moe_backward",
        )(*args)
        return gtok, gslot, gwin[None], gwout[None]

    in_specs = (
        P(None, "seq", "exp"),
        P(None, "seq", "exp"),
        P(None, None, "seq"),
        P(None, "exp"),
        P("exp", None, "seq"),
        P("exp", "seq", None),
    )
    out_specs = (
        P(None, "seq", "exp"),
        P(None, "exp"),
        P("exp", None, "seq"),
        P("exp", "seq", None),
    )
    return jax.shard_map(body, mesh=mesh, in_specs=in_specs, out_specs=out_specs, check_vma=False)
```

time: 1780 us -> 101 us (0.06)
  waiting for transfers between devices: 1030 us -> 0 us
  blocking collectives: 671 us -> 0 us
  Pallas kernels: 0 us -> 90.8 us
  other arithmetic: 24.7 us -> 0 us
    psum x3 -> x0, waiting for transfers between devices: 1000 us -> none  [the longest x1 425 us: body(): slot_in, slot_grad = lax.psum((slot_part, grad_part), 'seq')]
    psum x3 -> x0, blocking collectives: 375 us -> none  [the longest x1 197 us: body(): slot_in, slot_grad = lax.psum((slot_part, grad_part), 'seq')]
    all_gather x2 -> x0, blocking collectives: 211 us -> none  [merged(): pieces = jax.tree.map(lambda part: lax.all_gather(part, axis), value)]
    pallas_call x0 -> x1, Pallas kernels: none -> 90.8 us  [body(): pl.pallas_call(functools.partial(kernel, S, E, C), out_shape=outs, in_spe...]
    all_to_all x2 -> x0, blocking collectives: 85.4 us -> none  [the longest x1 45.3 us: body(): lax.all_to_all(slot_grad.astype(jnp.bfloat16), 'exp', split_axis=1, conca...]
    all_to_all x2 -> x0, waiting for transfers between devices: 26.3 us -> none  [the longest x1 13.8 us: body(): lax.all_to_all(out_part, 'exp', split_axis=2, concat_axis=1, tiled=True)]
    unnamed x2 -> x0, other arithmetic: 18.7 us -> none
  transfers between devices with their start and end apart: 5 -> 0, of which waited for: 5 -> 0; matrix products, arithmetic and copies ran while one was open for 0% -> 0% of each run, Pallas kernels for 0% -> 0%
where the time goes in v1:
time: 101 us; the launch traced here: 100 us
  Pallas kernels  90.8 us (90%)
  local copies, waits for them, and re-layouts  8.73 us (9%)
    pallas_call x1, Pallas kernels, body(): pl.pallas_call(functools.partial(kernel, S, E, C), out_shape=outs, in_spe...  90.8 us
    unnamed x16, local copies, waits for them, and re-layouts  8.73 us

profile of v1, /device:TPU:1, one launch (start us, length us, event | category | flops | bytes accessed | tf_op | source)
XLA Modules:
  0.0 100.2 jit_solution(9093295629359673858)
XLA Ops:
  0.6 0.0 copy-start
  0.6 1.0 %copy-done = bf16[8,256,128]{2,1,0:T(8,128)(2,1)S(1)} copy-done((bf16[8,256,128]{2,1,0:T(8,128)(2,1)S(1)}, bf16[8,256,128]{2,1,0:T(8,128)(2,1)}, u32[]{:S(2)}) %copy-start) | copy-done | bytes 524312
  1.7 0.0 copy-start.1
  1.7 1.0 %copy-done.1 = bf16[8,256,128]{2,1,0:T(8,128)(2,1)S(1)} copy-done((bf16[8,256,128]{2,1,0:T(8,128)(2,1)S(1)}, bf16[8,256,128]{2,1,0:T(8,128)(2,1)}, u32[]{:S(2)}) %copy-start.1) | copy-done | bytes 524312
  2.7 0.0 copy-start.2
  2.7 1.0 %copy-done.2 = bf16[1,2048,128]{2,1,0:T(8,128)(2,1)S(1)} copy-done((bf16[1,2048,128]{2,1,0:T(8,128)(2,1)S(1)}, bf16[1,2048,128]{2,1,0:T(8,128)(2,1)}, u32[]{:S(2)}) %copy-start.2) | copy-done | bytes 524312
  3.8 0.0 copy-start.3
  3.8 1.0 %copy-done.3 = bf16[1,128,2048]{2,1,0:T(8,128)(2,1)S(1)} copy-done((bf16[1,128,2048]{2,1,0:T(8,128)(2,1)S(1)}, bf16[1,128,2048]{2,1,0:T(8,128)(2,1)}, u32[]{:S(2)}) %copy-start.3) | copy-done | bytes 524312
  4.8 0.0 copy-start.4
  4.8 0.9 copy-done.4
  5.7 0.0 copy-start.5
  5.7 0.7 copy-done.5
  6.4 90.8 %moe_backward.1 = (bf16[8,256,128]{2,1,0:T(8,128)(2,1)S(1)}, f32[16,128]{1,0:T(8,128)S(1)}, bf16[2048,128]{1,0:T(8,128)(2,1)S(1)}, bf16[128,2048]{1,0:T(8,128)(2,1)S(1)}) custom-call(bf16[8,256,128]{2,1,0:T(8,128)(2,1)S(1)} %copy-done, bf16[8,256,128]{2,1,0:T(8,128)(2,1)S(1)} %copy-done.1, f32[8,16,256]{2,1,0:T(8,128)S(1)} %copy-done.4, ...), custom_call_target="tpu_custom_call" | custom-call | tf_op jit(solution)/shard_map/moe_backward/pallas_call | solution.py:356
  97.2 0.8 copy.14
  98.0 0.6 copy.15
  98.6 0.8 copy.16
  99.4 0.8 copy.17
Async XLA Ops:
  0.6 1.0 %copy-start = (bf16[8,256,128]{2,1,0:T(8,128)(2,1)S(1)}, bf16[8,256,128]{2,1,0:T(8,128)(2,1)}, u32[]{:S(2)}) copy-start(bf16[8,256,128]{2,1,0:T(8,128)(2,1)} %tokens_h.1) | copy-start | bytes 1572868
  1.7 1.0 %copy-start.1 = (bf16[8,256,128]{2,1,0:T(8,128)(2,1)S(1)}, bf16[8,256,128]{2,1,0:T(8,128)(2,1)}, u32[]{:S(2)}) copy-start(bf16[8,256,128]{2,1,0:T(8,128)(2,1)} %grad_h.1) | copy-start | bytes 1572868
  2.7 1.0 %copy-start.2 = (bf16[1,2048,128]{2,1,0:T(8,128)(2,1)S(1)}, bf16[1,2048,128]{2,1,0:T(8,128)(2,1)}, u32[]{:S(2)}) copy-start(bf16[1,2048,128]{2,1,0:T(8,128)(2,1)} %param.10) | copy-start | bytes 1572868
  3.8 1.0 %copy-start.3 = (bf16[1,128,2048]{2,1,0:T(8,128)(2,1)S(1)}, bf16[1,128,2048]{2,1,0:T(8,128)(2,1)}, u32[]{:S(2)}) copy-start(bf16[1,128,2048]{2,1,0:T(8,128)(2,1)} %param.11) | copy-start | bytes 1572868
  4.8 0.9 copy-start.4
  5.7 0.7 copy-start.5

commit v2 on v1

--- a/solution.py
+++ b/solution.py
@@ -48,6 +48,7 @@
     gtok, gslot, gwin, gwout,
     comb, disp,
     send1, recv1, send2, rows, send3, recv3, send4, recv4,
+    row1, rows1, row4, rows4, turned,
     send5, recv5, send6, recv6, recv7, recv8,
     slot_keep, lse_keep,
     in_sem, out_sem, send_sem, recv_sem,
@@ -109,8 +110,15 @@
     def keep(src, dst, k):
         pltpu.make_async_copy(src, dst, recv_sem.at[k]).start()
 
+    pending = []
+
     def sent(ref, k):
         wait_for(ref, send_sem.at[k])
+
+    def diagonal(count, shift):
+        down = lax.broadcasted_iota(jnp.int32, (count, 128), 0)
+        along = lax.broadcasted_iota(jnp.int32, (count, 128), 1)
+        return along == down + shift
 
     loads[0].wait()
     loads[1].wait()
@@ -128,9 +136,11 @@
         share = share / jnp.sum(share, axis=0, keepdims=True)
         comb[c] = share
         grad_parts.append(dot(share.astype(bf16), grad[c], 1, 0))
-    send1[:, 0:8, :] = jnp.swapaxes(jnp.stack(slot_parts), 0, 1)
-    send1[:, 8:16, :] = jnp.swapaxes(jnp.stack(grad_parts), 0, 1)
-    send1[:, 16:24, :] = jnp.swapaxes(jnp.stack(lse_parts), 0, 1)
+    send1[...] = jnp.concatenate(
+        [jnp.swapaxes(jnp.stack(slot_parts), 0, 1), jnp.swapaxes(jnp.stack(grad_parts), 0, 1)], axis=1
+    ).astype(bf16)
+    spread = jnp.swapaxes(jnp.stack(lse_parts), 0, 1).reshape(E * 8, 128)
+    row1[...] = jnp.sum(jnp.where(diagonal(E * 8, 0), spread, 0.0), axis=0, keepdims=True)
 
     flag = is_owner.astype(jnp.int32)
     pl.semaphore_wait(barrier, S - 1 + Q - 1 + 1 + E + flag * S - 2 * both.astype(jnp.int32))
@@ -141,29 +151,45 @@
 
         @pl.when(to != s)
         def _():
+            send(row1, rows1.at[pl.ds(s, 1)], 8, to, x)
             send(send1.at[e], recv1.at[s], 0, to, x)
 
         @pl.when(to == s)
         def _():
+            keep(row1, rows1.at[pl.ds(s, 1)], 8)
             keep(send1.at[e], recv1.at[s], 0)
 
     each(E, to_owner)
+
+    def sent_first():
+        sent(send1.at[pl.ds(0, E - 1)], 0)
+        each(E - 1, lambda i: sent(row1, 8))
+
+        @pl.when(jnp.logical_not(is_owner))
+        def _():
+            sent(send1.at[0], 0)
+            sent(row1, 8)
+
+    pending.append(sent_first)
 
     @pl.when(is_owner)
     def _():
+        wait_for(rows1, recv_sem.at[8])
+        turned[...] = jnp.transpose(rows1[...])
+        lses = turned[pl.ds(pl.multiple_of(mine * 8, 8), 8), :]
+        top = jnp.max(lses, axis=1, keepdims=True)
+        weights = jnp.exp(lses - top)
+        total = jnp.sum(weights, axis=1, keepdims=True)
+        weights = weights / total
+        lse_keep[...] = jnp.broadcast_to(top + jnp.log(total), (8, 128))
         wait_for(recv1, recv_sem.at[0])
-        top = lax.fori_loop(1, S, lambda i, t: jnp.maximum(t, recv1[i, 16:24, :]), recv1[0, 16:24, :])
-
-        def add(i, carry):
-            total, slots, grads = carry
-            weight = jnp.exp(recv1[i, 16:24, :] - top)
-            return total + weight, slots + weight * recv1[i, 0:8, :], grads + recv1[i, 8:16, :]
-
-        zero = jnp.zeros((8, 128), f32)
-        total, slots, grads = lax.fori_loop(0, S, add, (zero, zero, zero))
-        slots = slots / total
+        slots = jnp.zeros((8, 128), f32)
+        grads = jnp.zeros((8, 128), f32)
+        for i in range(S):
+            piece = recv1[i].astype(f32)
+            slots = slots + weights[:, i : i + 1] * piece[0:8]
+            grads = grads + piece[8:16]
         slot_keep[...] = slots
-        lse_keep[...] = top + jnp.log(total)
         send2[...] = jnp.concatenate([slots, grads], axis=0).astype(bf16)
 
         each(S - 1, lambda i: send(send2, rows.at[x], 1, lax.rem(s + 1 + i, S), mine))
@@ -176,6 +202,16 @@
         def _():
             keep(send2, rows.at[x], 1)
 
+    def sent_rows():
+        @pl.when(is_owner)
+        def _():
+            each(S - 1, lambda i: sent(send2, 1))
+
+            @pl.when(jnp.logical_not(both))
+            def _():
+                sent(send2, 1)
+
+    pending.append(sent_rows)
     loads[3].wait()
     loads[4].wait()
     wait_for(rows, recv_sem.at[1])
@@ -205,6 +241,15 @@
 
     each(E, to_home)
 
+    def sent_parts():
+        sent(send3.at[pl.ds(0, E - 1)], 2)
+
+        @pl.when(jnp.logical_not(both))
+        def _():
+            sent(send3.at[0], 2)
+
+    pending.append(sent_parts)
+
     blank = jnp.zeros((8, 128), f32)
     gwout[...] = dot(jnp.concatenate([blank, activated], axis=0).astype(bf16), held, 0, 0).astype(bf16)
     gwin[...] = dot(held, jnp.concatenate([pre_grad, blank], axis=0).astype(bf16), 0, 0).astype(bf16)
@@ -217,32 +262,50 @@
     def _():
         wait_for(recv3, recv_sem.at[2])
         total = lax.fori_loop(0, S, lambda i, t: t + recv3[i].astype(f32), jnp.zeros((16, 128), f32))
-        send4[0:16, :] = total
+        send4[...] = total.astype(bf16)
         stat = jnp.sum(total[8:16].astype(bf16).astype(f32) * slot_keep[...], axis=1, keepdims=True)
-        lane = lax.broadcasted_iota(jnp.int32, (8, 128), 1)
-        send4[16:24, :] = jnp.where(lane < 64, lse_keep[...], stat)
-        each(S - 1, lambda i: send(send4, recv4.at[mine], 3, lax.rem(s + 1 + i, S), x))
+        row4[...] = jnp.sum(
+            jnp.where(diagonal(8, 0), lse_keep[...], jnp.where(diagonal(8, 8), stat, 0.0)), axis=0, keepdims=True
+        )
+
+        def to_line(i):
+            to = lax.rem(s + 1 + i, S)
+            send(row4, rows4.at[pl.ds(mine, 1)], 9, to, x)
+            send(send4, recv4.at[mine], 3, to, x)
+
+        each(S - 1, to_line)
+        keep(row4, rows4.at[pl.ds(mine, 1)], 9)
         keep(send4, recv4.at[mine], 3)
 
+    def sent_sums():
+        @pl.when(is_owner)
+        def _():
+            each(S - 1, lambda i: sent(send4, 3))
+            each(S - 1, lambda i: sent(row4, 9))
+
+    pending.append(sent_sums)
     wait_for(recv4, recv_sem.at[3])
-    outs = jnp.swapaxes(recv4[:, 0:8, :], 0, 1)
-    backs = jnp.swapaxes(recv4[:, 8:16, :], 0, 1)
-    stats = jnp.swapaxes(recv4[:, 16:24, :], 0, 1)
+    wait_for(rows4, recv_sem.at[9])
+    sums = recv4[...].astype(f32)
+    outs = jnp.swapaxes(sums[:, 0:8, :], 0, 1).astype(bf16)
+    backs = jnp.swapaxes(sums[:, 8:16, :], 0, 1).astype(bf16)
+    scales = rows4[...]
     for c in range(C):
-        comb_grad = dot(outs[c].astype(bf16), grad[c], 1, 1)
-        disp_grad = dot(backs[c].astype(bf16), tokens[c], 1, 1)
-        dispatch = jnp.exp(logits[c] - stats[c][:, 0:1])
+        comb_grad = dot(outs[c], grad[c], 1, 1)
+        disp_grad = dot(backs[c], tokens[c], 1, 1)
+        dispatch = jnp.exp(logits[c] - scales[:, c : c + 1])
         share = comb[c]
         disp[c] = dispatch
         send5[c] = share * (
             comb_grad - jnp.sum(share * comb_grad, axis=0, keepdims=True)
-        ) + dispatch * (disp_grad - stats[c][:, 64:65])
+        ) + dispatch * (disp_grad - scales[:, C + c : C + c + 1])
 
     def to_peer(i):
         to = lax.rem(q + 1 + i, Q)
         send(send5.at[pl.ds(to * per, per)], recv5.at[q], 4, s, side + to)
 
     each(Q - 1, to_peer)
+    pending.append(lambda: sent(recv5.at[pl.ds(0, Q - 1)], 4))
     keep(send5.at[pl.ds(q * per, per)], recv5.at[q], 4)
     wait_for(recv5, recv_sem.at[4])
     part = recv5[0]
@@ -250,9 +313,11 @@
         part = part + recv5[i]
     send6[...] = part
     send(send6, recv6, 5, s, across)
+    pending.append(lambda: sent(send6, 5))
     wait_for(recv6, recv_sem.at[5])
     recv7[q] = (send6[...] + recv6[...]).astype(bf16)
     each(Q - 1, lambda i: send(recv7.at[q], recv7.at[q], 6, s, side + lax.rem(q + 1 + i, Q)))
+    pending.append(lambda: sent(recv7.at[pl.ds(0, Q - 1)], 6))
     loads[5].wait()
     wait_for(recv7.at[pl.ds(0, Q - 1)], recv_sem.at[6])
 
@@ -261,10 +326,11 @@
         term = term + dot(recv7[c // per, c % per], tokens[c], 1, 0)
     recv8[s] = term.astype(bf16)
     each(S - 1, lambda i: send(recv8.at[s], recv8.at[s], 7, lax.rem(s + 1 + i, S), x))
+    pending.append(lambda: sent(recv8.at[pl.ds(0, S - 1)], 7))
 
     for c in range(C):
         left = jnp.concatenate([disp[c].astype(bf16), recv7[c // per, c % per]], axis=0)
-        right = jnp.concatenate([backs[c].astype(bf16), params[...]], axis=0)
+        right = jnp.concatenate([backs[c], params[...]], axis=0)
         gtok[c] = dot(left, right, 0, 0).astype(bf16)
     store_tok = pltpu.make_async_copy(gtok, gtok_h, out_sem.at[2])
     store_tok.start()
@@ -277,36 +343,23 @@
     store_slot = pltpu.make_async_copy(gslot, gslot_h, out_sem.at[3])
     store_slot.start()
 
-    sent(send1.at[pl.ds(0, E - 1)], 0)
-
-    @pl.when(jnp.logical_not(is_owner))
-    def _():
-        sent(send1.at[0], 0)
-
-    @pl.when(is_owner)
-    def _():
-        each(S - 1, lambda i: sent(send2, 1))
-
-        @pl.when(jnp.logical_not(both))
-        def _():
-            sent(send2, 1)
-
-        each(S - 1, lambda i: sent(send4, 3))
-
-    sent(send3.at[pl.ds(0, E - 1)], 2)
-
-    @pl.when(jnp.logical_not(both))
-    def _():
-        sent(send3.at[0], 2)
-
-    sent(recv5.at[pl.ds(0, Q - 1)], 4)
-    sent(send6, 5)
-    sent(recv7.at[pl.ds(0, Q - 1)], 6)
-    sent(recv8.at[pl.ds(0, S - 1)], 7)
+    for wait in pending:
+        wait()
     store_out.wait()
     store_in.wait()
     store_tok.wait()
     store_slot.wait()
+
+
+def hand_over(a, b, c, d, to_a, to_b, to_c, to_d, sem):
+    copies = [
+        pltpu.make_async_copy(src, dst, sem.at[i])
+        for i, (src, dst) in enumerate(((a, to_a), (b, to_b), (c, to_c), (d, to_d)))
+    ]
+    for copy in copies:
+        copy.start()
+    for copy in copies:
+        copy.wait()
 
 
 def solution(mesh):
@@ -331,14 +384,19 @@
             + [
                 pltpu.VMEM((C, E, M), f32),
                 pltpu.VMEM((C, E, M), f32),
-                pltpu.VMEM((E, 24, D), f32),
-                pltpu.VMEM((S, 24, D), f32),
+                pltpu.VMEM((E, 16, D), bf16),
+                pltpu.VMEM((S, 16, D), bf16),
                 pltpu.VMEM((16, D), bf16),
                 pltpu.VMEM((E, 16, D), bf16),
                 pltpu.VMEM((E, 16, D), bf16),
                 pltpu.VMEM((S, 16, D), bf16),
-                pltpu.VMEM((24, D), f32),
-                pltpu.VMEM((E, 24, D), f32),
+                pltpu.VMEM((16, D), bf16),
+                pltpu.VMEM((E, 16, D), bf16),
+                pltpu.VMEM((1, 128), f32),
+                pltpu.VMEM((S, 128), f32),
+                pltpu.VMEM((1, 128), f32),
+                pltpu.VMEM((E, 128), f32),
+                pltpu.VMEM((128, S), f32),
                 pltpu.VMEM((C, E, M), f32),
                 pltpu.VMEM((Q, per, E, M), f32),
                 pltpu.VMEM((per, E, M), f32),
@@ -349,8 +407,8 @@
                 pltpu.VMEM((8, D), f32),
                 pltpu.SemaphoreType.DMA((6,)),
                 pltpu.SemaphoreType.DMA((4,)),
-                pltpu.SemaphoreType.DMA((8,)),
-                pltpu.SemaphoreType.DMA((8,)),
+                pltpu.SemaphoreType.DMA((10,)),
+                pltpu.SemaphoreType.DMA((10,)),
             ]
         )
         gtok, gslot, gwin, gwout = pl.pallas_call(
@@ -360,10 +418,18 @@
             out_specs=[pl.BlockSpec(memory_space=pl.ANY)] * 4,
             scratch_shapes=scratch,
             compiler_params=pltpu.CompilerParams(
-                collective_id=0, has_side_effects=True, vmem_limit_bytes=48 << 20
+                collective_id=0, has_side_effects=True, vmem_limit_bytes=60 << 20
             ),
             name="moe_backward",
         )(*args)
+        gtok, gslot, gwin, gwout = pl.pallas_call(
+            hand_over,
+            out_shape=outs,
+            in_specs=[pl.BlockSpec(memory_space=pl.ANY)] * 4,
+            out_specs=[pl.BlockSpec(memory_space=pl.ANY)] * 4,
+            scratch_shapes=[pltpu.SemaphoreType.DMA((4,))],
+            name="hand_over",
+        )(gtok, gslot, gwin, gwout)
         return gtok, gslot, gwin[None], gwout[None]
 
     in_specs = (

time: 101 us -> 130 us (1.29)
  Pallas kernels: 90.8 us -> 129 us
  local copies, waits for them, and re-layouts: 8.73 us -> 0 us
    pallas_call x0 -> x1, Pallas kernels: none -> 49 us  [body(): pl.pallas_call(hand_over, out_shape=outs, in_specs=[pl.BlockSpec(memory_s...]
    pallas_call x1, Pallas kernels: 90.8 us -> 80.5 us  [body(): pl.pallas_call(functools.partial(kernel, S, E, C), out_shape=outs, in_spe...]
    unnamed x16 -> x0, local copies, waits for them, and re-layouts: 8.73 us -> none
where the time goes in v2:
time: 130 us
  Pallas kernels  129 us (99%)
    pallas_call x1, Pallas kernels, body(): pl.pallas_call(functools.partial(kernel, S, E, C), out_shape=outs, in_spe...  80.5 us
    pallas_call x1, Pallas kernels, body(): pl.pallas_call(hand_over, out_shape=outs, in_specs=[pl.BlockSpec(memory_s...  49 us

profile of v2, /device:TPU:1, one launch (start us, length us, event | category | flops | bytes accessed | tf_op | source)
XLA Modules:
  0.0 130.1 jit_solution(16331363042497312455)
XLA Ops:
  0.6 80.5 %moe_backward.1 = (bf16[8,256,128]{2,1,0:T(8,128)(2,1)}, f32[16,128]{1,0:T(8,128)}, bf16[2048,128]{1,0:T(8,128)(2,1)}, bf16[128,2048]{1,0:T(8,128)(2,1)}) custom-call(bf16[8,256,128]{2,1,0:T(8,128)(2,1)} %tokens_h.1, bf16[8,256,128]{2,1,0:T(8,128)(2,1)} %grad_h.1, f32[8,16,256]{2,1,0:T(8,128)} %logits_h.1, bf16[16,128]{1,0:T(8,128)(2,1)} %params_h.1, ...), custom_call_target="tpu_custom_call" | custom-call | tf_op jit(solution)/shard_map/moe_backward/pallas_call | solution.py:414
  81.1 49.0 %hand_over.1 = (bf16[8,256,128]{2,1,0:T(8,128)(2,1)}, f32[16,128]{1,0:T(8,128)}, bf16[2048,128]{1,0:T(8,128)(2,1)}, bf16[128,2048]{1,0:T(8,128)(2,1)}) custom-call(bf16[8,256,128]{2,1,0:T(8,128)(2,1)} %get-tuple-element.12.a, f32[16,128]{1,0:T(8,128)} %get-tuple-element.13.b, bf16[2048,128]{1,0:T(8,128)(2,1)} %get-tuple-element.14.c, ...), custom_call_target="tpu_custom_call" | custom-call | tf_op jit(solution)/shard_map/hand_over/pallas_call | solution.py:425

commit v3 on v2

--- a/solution.py
+++ b/solution.py
@@ -51,7 +51,7 @@
     row1, rows1, row4, rows4, turned,
     send5, recv5, send6, recv6, recv7, recv8,
     slot_keep, lse_keep,
-    in_sem, out_sem, send_sem, recv_sem,
+    in_sem, out_sem, send_sem, recv_sem, go_sem,
 ):
     s = lax.axis_index("seq")
     x = lax.axis_index("exp")
@@ -84,22 +84,23 @@
     def greet(ds, dx):
         pl.semaphore_signal(barrier, inc=1, device_id=(ds, dx), device_id_type=MESH)
 
-    each(S - 1, lambda i: greet(lax.rem(s + 1 + i, S), x))
-    each(Q - 1, lambda i: greet(s, side + lax.rem(q + 1 + i, Q)))
-    greet(s, across)
-    each(E - 1, lambda i: greet(home, lax.rem(x + 1 + i, E)))
-
-    @pl.when(jnp.logical_not(both))
-    def _():
-        greet(home, x)
-
     @pl.when(is_owner)
     def _():
-        each(S - 1, lambda i: greet(lax.rem(s + 1 + i, S), mine))
-
-        @pl.when(jnp.logical_not(both))
-        def _():
-            greet(s, mine)
+        def to_rest(i):
+            k = lax.rem(i + s, S - E)
+            zz = lax.rem(k, half)
+            greet(lax.div(k, half) * LINE + jnp.where(zz < LINE // 4, zz, zz + half), x)
+
+        each(S - E, to_rest)
+
+    def to_far(i):
+        to = lax.rem(x + Q + i, E)
+
+        @pl.when(jnp.logical_or(jnp.logical_not(both), to != x))
+        def _():
+            greet(home, to)
+
+    each(E, to_far)
 
     def send(src, dst, k, ds, dx):
         pltpu.make_async_remote_copy(
@@ -142,8 +143,15 @@
     spread = jnp.swapaxes(jnp.stack(lse_parts), 0, 1).reshape(E * 8, 128)
     row1[...] = jnp.sum(jnp.where(diagonal(E * 8, 0), spread, 0.0), axis=0, keepdims=True)
 
-    flag = is_owner.astype(jnp.int32)
-    pl.semaphore_wait(barrier, S - 1 + Q - 1 + 1 + E + flag * S - 2 * both.astype(jnp.int32))
+    @pl.when(jnp.logical_not(is_owner))
+    def _():
+        pl.semaphore_wait(barrier, E)
+        near = jnp.where(z < LINE // 4, half - 1 - z, 3 * half - 1 - z)
+        pl.semaphore_signal(go_sem, inc=1, device_id=(s - z + near, x), device_id_type=MESH)
+
+    @pl.when(is_owner)
+    def _():
+        pl.semaphore_wait(go_sem, 1)
 
     def to_owner(i):
         e = lax.rem(x + s + i, E)
@@ -192,6 +200,7 @@
         slot_keep[...] = slots
         send2[...] = jnp.concatenate([slots, grads], axis=0).astype(bf16)
 
+        pl.semaphore_wait(barrier, S - both.astype(jnp.int32))
         each(S - 1, lambda i: send(send2, rows.at[x], 1, lax.rem(s + 1 + i, S), mine))
 
         @pl.when(jnp.logical_not(both))
@@ -296,9 +305,10 @@
         dispatch = jnp.exp(logits[c] - scales[:, c : c + 1])
         share = comb[c]
         disp[c] = dispatch
-        send5[c] = share * (
+        part = share * (
             comb_grad - jnp.sum(share * comb_grad, axis=0, keepdims=True)
         ) + dispatch * (disp_grad - scales[:, C + c : C + c + 1])
+        send5[c] = part.astype(bf16)
 
     def to_peer(i):
         to = lax.rem(q + 1 + i, Q)
@@ -308,9 +318,9 @@
     pending.append(lambda: sent(recv5.at[pl.ds(0, Q - 1)], 4))
     keep(send5.at[pl.ds(q * per, per)], recv5.at[q], 4)
     wait_for(recv5, recv_sem.at[4])
-    part = recv5[0]
+    part = recv5[0].astype(f32)
     for i in range(1, Q):
-        part = part + recv5[i]
+        part = part + recv5[i].astype(f32)
     send6[...] = part
     send(send6, recv6, 5, s, across)
     pending.append(lambda: sent(send6, 5))
@@ -351,14 +361,16 @@
     store_slot.wait()
 
 
-def hand_over(a, b, c, d, to_a, to_b, to_c, to_d, sem):
-    copies = [
-        pltpu.make_async_copy(src, dst, sem.at[i])
-        for i, (src, dst) in enumerate(((a, to_a), (b, to_b), (c, to_c), (d, to_d)))
-    ]
-    for copy in copies:
+def hand_over(*refs):
+    sources, targets, held, sem = refs[0:4], refs[4:8], refs[8:12], refs[12]
+    ins = [pltpu.make_async_copy(sources[i], held[i], sem.at[i]) for i in range(4)]
+    outs = [pltpu.make_async_copy(held[i], targets[i], sem.at[4 + i]) for i in range(4)]
+    for copy in ins:
         copy.start()
-    for copy in copies:
+    for i in range(4):
+        ins[i].wait()
+        outs[i].start()
+    for copy in outs:
         copy.wait()
 
 
@@ -397,8 +409,8 @@
                 pltpu.VMEM((1, 128), f32),
                 pltpu.VMEM((E, 128), f32),
                 pltpu.VMEM((128, S), f32),
-                pltpu.VMEM((C, E, M), f32),
-                pltpu.VMEM((Q, per, E, M), f32),
+                pltpu.VMEM((C, E, M), bf16),
+                pltpu.VMEM((Q, per, E, M), bf16),
                 pltpu.VMEM((per, E, M), f32),
                 pltpu.VMEM((per, E, M), f32),
                 pltpu.VMEM((Q, per, E, M), bf16),
@@ -409,12 +421,13 @@
                 pltpu.SemaphoreType.DMA((4,)),
                 pltpu.SemaphoreType.DMA((10,)),
                 pltpu.SemaphoreType.DMA((10,)),
+                pltpu.SemaphoreType.REGULAR,
             ]
         )
         gtok, gslot, gwin, gwout = pl.pallas_call(
             functools.partial(kernel, S, E, C),
             out_shape=outs,
-            in_specs=[pl.BlockSpec(memory_space=pl.ANY)] * 6,
+            in_specs=[pl.BlockSpec(memory_space=pltpu.HBM)] * 6,
             out_specs=[pl.BlockSpec(memory_space=pl.ANY)] * 4,
             scratch_shapes=scratch,
             compiler_params=pltpu.CompilerParams(
@@ -426,8 +439,8 @@
             hand_over,
             out_shape=outs,
             in_specs=[pl.BlockSpec(memory_space=pl.ANY)] * 4,
-            out_specs=[pl.BlockSpec(memory_space=pl.ANY)] * 4,
-            scratch_shapes=[pltpu.SemaphoreType.DMA((4,))],
+            out_specs=[pl.BlockSpec(memory_space=pltpu.HBM)] * 4,
+            scratch_shapes=[hold(a) for a in outs] + [pltpu.SemaphoreType.DMA((8,))],
             name="hand_over",
         )(gtok, gslot, gwin, gwout)
         return gtok, gslot, gwin[None], gwout[None]

time: 130 us -> 81.4 us (0.63)
  Pallas kernels: 129 us -> 79.9 us
    pallas_call x1, Pallas kernels: 49 us -> 2.25 us  [body(): pl.pallas_call(hand_over, out_shape=outs, in_specs=[pl.BlockSpec(memory_s...]
    pallas_call x1, Pallas kernels: 80.5 us -> 77.7 us  [body(): pl.pallas_call(functools.partial(kernel, S, E, C), out_shape=outs, in_spe...]
where the time goes in v3:
time: 81.4 us; the launch traced here: 80.6 us
  Pallas kernels  79.9 us (98%)
    pallas_call x1, Pallas kernels, body(): pl.pallas_call(functools.partial(kernel, S, E, C), out_shape=outs, in_spe...  77.7 us
    pallas_call x1, Pallas kernels, body(): pl.pallas_call(hand_over, out_shape=outs, in_specs=[pl.BlockSpec(memory_s...  2.25 us

profile of v3, /device:TPU:1, one launch (start us, length us, event | category | flops | bytes accessed | tf_op | source)
XLA Modules:
  0.0 80.6 jit_solution(10248181654046834955)
XLA Ops:
  0.6 77.7 %moe_backward.1 = (bf16[8,256,128]{2,1,0:T(8,128)(2,1)}, f32[16,128]{1,0:T(8,128)}, bf16[2048,128]{1,0:T(8,128)(2,1)}, bf16[128,2048]{1,0:T(8,128)(2,1)}) custom-call(bf16[8,256,128]{2,1,0:T(8,128)(2,1)} %tokens_h.1, bf16[8,256,128]{2,1,0:T(8,128)(2,1)} %grad_h.1, f32[8,16,256]{2,1,0:T(8,128)} %logits_h.1, bf16[16,128]{1,0:T(8,128)(2,1)} %params_h.1, ...), custom_call_target="tpu_custom_call" | custom-call | tf_op jit(solution)/shard_map/moe_backward/pallas_call | solution.py:427
  78.3 2.3 %hand_over.1 = (bf16[8,256,128]{2,1,0:T(8,128)(2,1)}, f32[16,128]{1,0:T(8,128)}, bf16[2048,128]{1,0:T(8,128)(2,1)}, bf16[128,2048]{1,0:T(8,128)(2,1)}) custom-call(bf16[8,256,128]{2,1,0:T(8,128)(2,1)} %get-tuple-element.12.refs_0_, f32[16,128]{1,0:T(8,128)} %get-tuple-element.13.refs_1_, bf16[2048,128]{1,0:T(8,128)(2,1)} %get-tuple-element.14.refs_2_, ...), custom_call_target="tpu_custom_call" | custom-call | tf_op jit(solution)/shard_map/hand_over/pallas_call | solution.py:438

commit v4 on v3

--- a/solution.py
+++ b/solution.py
@@ -66,6 +66,21 @@
         return lax.div(e, half) * LINE + LINE // 4 + lax.rem(e, half)
 
     z = lax.rem(s, LINE)
+    lines = S // LINE
+
+    def swing(i):
+        return jnp.where(lax.rem(i, 2) == 1, lax.div(i + 1, 2), -lax.div(i + 1, 2))
+
+    def far_line(i):
+        return lax.rem(lax.div(s, LINE) + lines // 2 + swing(lax.rem(i, lines)) + lines, lines)
+
+    def far_ring(i, start):
+        return far_line(i) * LINE + lax.rem(z + start + swing(lax.div(i, lines)) + LINE, LINE)
+
+    def far_end(i):
+        k = lax.div(i, lines)
+        return far_line(i) * LINE + jnp.where(z < half, LINE - 1 - k, k)
+
     is_owner = jnp.logical_and(z >= LINE // 4, z < LINE // 4 + half)
     mine = lax.div(s, LINE) * half + jnp.clip(z - LINE // 4, 0, half - 1)
     both = jnp.logical_and(is_owner, mine == x)
@@ -146,15 +161,27 @@
     @pl.when(jnp.logical_not(is_owner))
     def _():
         pl.semaphore_wait(barrier, E)
-        near = jnp.where(z < LINE // 4, half - 1 - z, 3 * half - 1 - z)
-        pl.semaphore_signal(go_sem, inc=1, device_id=(s - z + near, x), device_id_type=MESH)
+
+        def go(first):
+            for i in range(half // 2):
+                to = s - z + first + i
+                pl.semaphore_signal(go_sem, inc=1, device_id=(to, x), device_id_type=MESH)
+
+        @pl.when(z == LINE // 4 - 1)
+        def _():
+            go(LINE // 4)
+
+        @pl.when(z == LINE // 4 + half)
+        def _():
+            go(LINE // 4 + half // 2)
 
     @pl.when(is_owner)
     def _():
         pl.semaphore_wait(go_sem, 1)
 
     def to_owner(i):
-        e = lax.rem(x + s + i, E)
+        k = lax.div(i, lines)
+        e = far_line(i) * half + jnp.where(z < half, half - 1 - k, k)
         to = owner(e)
 
         @pl.when(to != s)
@@ -201,15 +228,21 @@
         send2[...] = jnp.concatenate([slots, grads], axis=0).astype(bf16)
 
         pl.semaphore_wait(barrier, S - both.astype(jnp.int32))
-        each(S - 1, lambda i: send(send2, rows.at[x], 1, lax.rem(s + 1 + i, S), mine))
-
-        @pl.when(jnp.logical_not(both))
-        def _():
-            send(send2, rows.at[x], 1, s, mine)
-
-        @pl.when(both)
-        def _():
-            keep(send2, rows.at[x], 1)
+        start = jnp.where(lax.div(mine, Q) == lax.div(x, Q), half, 0)
+
+        def to_expert(i):
+            to = far_ring(i, start)
+            own = jnp.logical_and(both, to == s)
+
+            @pl.when(jnp.logical_not(own))
+            def _():
+                send(send2, rows.at[x], 1, to, mine)
+
+            @pl.when(own)
+            def _():
+                keep(send2, rows.at[x], 1)
+
+        each(S, to_expert)
 
     def sent_rows():
         @pl.when(is_owner)
@@ -237,7 +270,7 @@
         send3[i] = jnp.concatenate([out_part[0:8, cut], back_part[8:16, cut]], axis=0).astype(bf16)
 
     def to_home(i):
-        to = lax.rem(x + s + i, E)
+        to = jnp.where(i < Q, Q - side, side) + lax.rem(q + Q // 2 + swing(lax.rem(i, Q)) + Q, Q)
         own = jnp.logical_and(both, to == x)
 
         @pl.when(jnp.logical_not(own))
@@ -278,7 +311,7 @@
         )
 
         def to_line(i):
-            to = lax.rem(s + 1 + i, S)
+            to = far_ring(i, half)
             send(row4, rows4.at[pl.ds(mine, 1)], 9, to, x)
             send(send4, recv4.at[mine], 3, to, x)
 
@@ -331,11 +364,18 @@
     loads[5].wait()
     wait_for(recv7.at[pl.ds(0, Q - 1)], recv_sem.at[6])
 
-    term = jnp.zeros((E, 128), f32)
-    for c in range(C):
-        term = term + dot(recv7[c // per, c % per], tokens[c], 1, 0)
+    wide = jnp.concatenate([recv7[c // per, c % per] for c in range(C)], axis=1)
+    term = dot(wide, tokens[...].reshape(wide.shape[1], 128), 1, 0)
     recv8[s] = term.astype(bf16)
-    each(S - 1, lambda i: send(recv8.at[s], recv8.at[s], 7, lax.rem(s + 1 + i, S), x))
+
+    def to_plane(i):
+        to = far_end(i)
+
+        @pl.when(to != s)
+        def _():
+            send(recv8.at[s], recv8.at[s], 7, to, x)
+
+    each(S, to_plane)
     pending.append(lambda: sent(recv8.at[pl.ds(0, S - 1)], 7))
 
     for c in range(C):

time: 81.4 us -> 78.9 us (0.969)
  Pallas kernels: 79.9 us -> 77.7 us
    pallas_call x1, Pallas kernels: 77.7 us -> 75.5 us  [body(): pl.pallas_call(functools.partial(kernel, S, E, C), out_shape=outs, in_spe...]
where the time goes in v4:
time: 78.9 us; the launch traced here: 78.4 us
  Pallas kernels  77.7 us (98%)
    pallas_call x1, Pallas kernels, body(): pl.pallas_call(functools.partial(kernel, S, E, C), out_shape=outs, in_spe...  75.5 us
    pallas_call x1, Pallas kernels, body(): pl.pallas_call(hand_over, out_shape=outs, in_specs=[pl.BlockSpec(memory_s...  2.25 us

profile of v4, /device:TPU:1, one launch (start us, length us, event | category | flops | bytes accessed | tf_op | source)
XLA Modules:
  0.0 78.4 jit_solution(6683893293509162931)
XLA Ops:
  0.6 75.5 %moe_backward.1 = (bf16[8,256,128]{2,1,0:T(8,128)(2,1)}, f32[16,128]{1,0:T(8,128)}, bf16[2048,128]{1,0:T(8,128)(2,1)}, bf16[128,2048]{1,0:T(8,128)(2,1)}) custom-call(bf16[8,256,128]{2,1,0:T(8,128)(2,1)} %tokens_h.1, bf16[8,256,128]{2,1,0:T(8,128)(2,1)} %grad_h.1, f32[8,16,256]{2,1,0:T(8,128)} %logits_h.1, bf16[16,128]{1,0:T(8,128)(2,1)} %params_h.1, ...), custom_call_target="tpu_custom_call" | custom-call | tf_op jit(solution)/shard_map/moe_backward/pallas_call | solution.py:467
  76.1 2.3 %hand_over.1 = (bf16[8,256,128]{2,1,0:T(8,128)(2,1)}, f32[16,128]{1,0:T(8,128)}, bf16[2048,128]{1,0:T(8,128)(2,1)}, bf16[128,2048]{1,0:T(8,128)(2,1)}) custom-call(bf16[8,256,128]{2,1,0:T(8,128)(2,1)} %get-tuple-element.12.refs_0_, f32[16,128]{1,0:T(8,128)} %get-tuple-element.13.refs_1_, bf16[2048,128]{1,0:T(8,128)(2,1)} %get-tuple-element.14.refs_2_, ...), custom_call_target="tpu_custom_call" | custom-call | tf_op jit(solution)/shard_map/hand_over/pallas_call | solution.py:478

commit v5 on v4

--- a/solution.py
+++ b/solution.py
@@ -49,7 +49,7 @@
     comb, disp,
     send1, recv1, send2, rows, send3, recv3, send4, recv4,
     row1, rows1, row4, rows4, turned,
-    send5, recv5, send6, recv6, recv7, recv8,
+    send5, pair, summed, recv5, recv7, recv8,
     slot_keep, lse_keep,
     in_sem, out_sem, send_sem, recv_sem, go_sem,
 ):
@@ -86,6 +86,29 @@
     both = jnp.logical_and(is_owner, mine == x)
     home = owner(x)
 
+    barrier = pltpu.get_barrier_semaphore()
+
+    def greet(ds, dx):
+        pl.semaphore_signal(barrier, inc=1, device_id=(ds, dx), device_id_type=MESH)
+
+    @pl.when(is_owner)
+    def _():
+        def to_rest(i):
+            k = lax.rem(i + s, S - E)
+            zz = lax.rem(k, half)
+            greet(lax.div(k, half) * LINE + jnp.where(zz < LINE // 4, zz, zz + half), x)
+
+        each(S - E, to_rest)
+
+    def to_far(i):
+        to = lax.rem(x + Q + i, E)
+
+        @pl.when(jnp.logical_or(jnp.logical_not(both), to != x))
+        def _():
+            greet(home, to)
+
+    each(E, to_far)
+
     loads = []
     for i, (a, b) in enumerate(
         ((logits_h, logits), (tokens_h, tokens), (grad_h, grad), (win_h, win), (wout_h, wout), (params_h, params))
@@ -93,29 +116,6 @@
         copy = pltpu.make_async_copy(a, b, in_sem.at[i])
         copy.start()
         loads.append(copy)
-
-    barrier = pltpu.get_barrier_semaphore()
-
-    def greet(ds, dx):
-        pl.semaphore_signal(barrier, inc=1, device_id=(ds, dx), device_id_type=MESH)
-
-    @pl.when(is_owner)
-    def _():
-        def to_rest(i):
-            k = lax.rem(i + s, S - E)
-            zz = lax.rem(k, half)
-            greet(lax.div(k, half) * LINE + jnp.where(zz < LINE // 4, zz, zz + half), x)
-
-        each(S - E, to_rest)
-
-    def to_far(i):
-        to = lax.rem(x + Q + i, E)
-
-        @pl.when(jnp.logical_or(jnp.logical_not(both), to != x))
-        def _():
-            greet(home, to)
-
-    each(E, to_far)
 
     def send(src, dst, k, ds, dx):
         pltpu.make_async_remote_copy(
@@ -303,7 +303,10 @@
     @pl.when(is_owner)
     def _():
         wait_for(recv3, recv_sem.at[2])
-        total = lax.fori_loop(0, S, lambda i, t: t + recv3[i].astype(f32), jnp.zeros((16, 128), f32))
+        sums = [recv3[i].astype(f32) for i in range(4)]
+        for i in range(4, S):
+            sums[i % 4] = sums[i % 4] + recv3[i].astype(f32)
+        total = (sums[0] + sums[1]) + (sums[2] + sums[3])
         send4[...] = total.astype(bf16)
         stat = jnp.sum(total[8:16].astype(bf16).astype(f32) * slot_keep[...], axis=1, keepdims=True)
         row4[...] = jnp.sum(
@@ -341,24 +344,32 @@
         part = share * (
             comb_grad - jnp.sum(share * comb_grad, axis=0, keepdims=True)
         ) + dispatch * (disp_grad - scales[:, C + c : C + c + 1])
-        send5[c] = part.astype(bf16)
+        chunk = c // per
+        send5[(chunk % 2 * (Q // 2) + chunk // 2) * per + c % per] = part.astype(bf16)
+
+    core = lax.rem(x, 2)
+    deep = C // 2
+    pieces = Q // 2
+    send(send5.at[pl.ds((1 - core) * deep, deep)], pair, 5, s, x + 1 - 2 * core)
+    pending.append(lambda: sent(pair, 5))
+    wait_for(pair, recv_sem.at[5])
+    for i in range(pieces):
+        own = send5[pl.ds(core * deep + i * per, per)].astype(f32)
+        summed[i] = (own + pair[i * per : i * per + per].astype(f32)).astype(bf16)
+    slot = lax.div(x, 2)
 
     def to_peer(i):
-        to = lax.rem(q + 1 + i, Q)
-        send(send5.at[pl.ds(to * per, per)], recv5.at[q], 4, s, side + to)
+        to = lax.rem(lax.div(q, 2) + pieces // 2 + swing(lax.rem(i, pieces)) + pieces, pieces)
+        send(summed.at[to], recv5.at[slot], 4, s, jnp.where(i < pieces, Q - side, side) + 2 * to + core)
 
     each(Q - 1, to_peer)
     pending.append(lambda: sent(recv5.at[pl.ds(0, Q - 1)], 4))
-    keep(send5.at[pl.ds(q * per, per)], recv5.at[q], 4)
+    keep(summed.at[lax.div(q, 2)], recv5.at[slot], 4)
     wait_for(recv5, recv_sem.at[4])
     part = recv5[0].astype(f32)
     for i in range(1, Q):
         part = part + recv5[i].astype(f32)
-    send6[...] = part
-    send(send6, recv6, 5, s, across)
-    pending.append(lambda: sent(send6, 5))
-    wait_for(recv6, recv_sem.at[5])
-    recv7[q] = (send6[...] + recv6[...]).astype(bf16)
+    recv7[q] = part.astype(bf16)
     each(Q - 1, lambda i: send(recv7.at[q], recv7.at[q], 6, s, side + lax.rem(q + 1 + i, Q)))
     pending.append(lambda: sent(recv7.at[pl.ds(0, Q - 1)], 6))
     loads[5].wait()
@@ -376,7 +387,6 @@
             send(recv8.at[s], recv8.at[s], 7, to, x)
 
     each(S, to_plane)
-    pending.append(lambda: sent(recv8.at[pl.ds(0, S - 1)], 7))
 
     for c in range(C):
         left = jnp.concatenate([disp[c].astype(bf16), recv7[c // per, c % per]], axis=0)
@@ -385,6 +395,11 @@
     store_tok = pltpu.make_async_copy(gtok, gtok_h, out_sem.at[2])
     store_tok.start()
 
+    for wait in pending:
+        wait()
+    store_out.wait()
+    store_in.wait()
+    store_tok.wait()
     wait_for(recv8.at[pl.ds(0, S - 1)], recv_sem.at[7])
     total = recv8[0].astype(f32)
     for i in range(1, S):
@@ -393,11 +408,7 @@
     store_slot = pltpu.make_async_copy(gslot, gslot_h, out_sem.at[3])
     store_slot.start()
 
-    for wait in pending:
-        wait()
-    store_out.wait()
-    store_in.wait()
-    store_tok.wait()
+    sent(recv8.at[pl.ds(0, S - 1)], 7)
     store_slot.wait()
 
 
@@ -450,9 +461,9 @@
                 pltpu.VMEM((E, 128), f32),
                 pltpu.VMEM((128, S), f32),
                 pltpu.VMEM((C, E, M), bf16),
+                pltpu.VMEM((C // 2, E, M), bf16),
+                pltpu.VMEM((Q // 2, per, E, M), bf16),
                 pltpu.VMEM((Q, per, E, M), bf16),
-                pltpu.VMEM((per, E, M), f32),
-                pltpu.VMEM((per, E, M), f32),
                 pltpu.VMEM((Q, per, E, M), bf16),
                 pltpu.VMEM((S, E, D), bf16),
                 pltpu.VMEM((8, D), f32),

time: 78.9 us -> 78.1 us (0.990)
  no operation moved by 1% of the time
where the time goes in v5:
time: 78.1 us; the launch traced here: 77.9 us
  Pallas kernels  77.3 us (99%)
    pallas_call x1, Pallas kernels, body(): pl.pallas_call(functools.partial(kernel, S, E, C), out_shape=outs, in_spe...  75 us
    pallas_call x1, Pallas kernels, body(): pl.pallas_call(hand_over, out_shape=outs, in_specs=[pl.BlockSpec(memory_s...  2.25 us

profile of v5, /device:TPU:1, one launch (start us, length us, event | category | flops | bytes accessed | tf_op | source)
XLA Modules:
  0.0 77.9 jit_solution(16729131920213044906)
XLA Ops:
  0.6 75.0 %moe_backward.1 = (bf16[8,256,128]{2,1,0:T(8,128)(2,1)}, f32[16,128]{1,0:T(8,128)}, bf16[2048,128]{1,0:T(8,128)(2,1)}, bf16[128,2048]{1,0:T(8,128)(2,1)}) custom-call(bf16[8,256,128]{2,1,0:T(8,128)(2,1)} %tokens_h.1, bf16[8,256,128]{2,1,0:T(8,128)(2,1)} %grad_h.1, f32[8,16,256]{2,1,0:T(8,128)} %logits_h.1, bf16[16,128]{1,0:T(8,128)(2,1)} %params_h.1, ...), custom_call_target="tpu_custom_call" | custom-call | tf_op jit(solution)/shard_map/moe_backward/pallas_call | solution.py:478
  75.7 2.3 %hand_over.1 = (bf16[8,256,128]{2,1,0:T(8,128)(2,1)}, f32[16,128]{1,0:T(8,128)}, bf16[2048,128]{1,0:T(8,128)(2,1)}, bf16[128,2048]{1,0:T(8,128)(2,1)}) custom-call(bf16[8,256,128]{2,1,0:T(8,128)(2,1)} %get-tuple-element.12.refs_0_, f32[16,128]{1,0:T(8,128)} %get-tuple-element.13.refs_1_, bf16[2048,128]{1,0:T(8,128)(2,1)} %get-tuple-element.14.refs_2_, ...), custom_call_target="tpu_custom_call" | custom-call | tf_op jit(solution)/shard_map/hand_over/pallas_call | solution.py:489

commit v6 on v5

--- a/solution.py
+++ b/solution.py
@@ -43,13 +43,13 @@
 def kernel(
     S, E, C,
     tokens_h, grad_h, logits_h, params_h, win_h, wout_h,
-    gtok_h, gslot_h, gwin_h, gwout_h,
+    gtok_h, recv8, gwin_h, gwout_h,
     tokens, grad, logits, params, win, wout,
-    gtok, gslot, gwin, gwout,
+    gtok, term8, gwin, gwout,
     comb, disp,
     send1, recv1, send2, rows, send3, recv3, send4, recv4,
     row1, rows1, row4, rows4, turned,
-    send5, pair, summed, recv5, recv7, recv8,
+    send5, pair, summed, recv5, recv7,
     slot_keep, lse_keep,
     in_sem, out_sem, send_sem, recv_sem, go_sem,
 ):
@@ -370,21 +370,25 @@
     for i in range(1, Q):
         part = part + recv5[i].astype(f32)
     recv7[q] = part.astype(bf16)
-    each(Q - 1, lambda i: send(recv7.at[q], recv7.at[q], 6, s, side + lax.rem(q + 1 + i, Q)))
+    each(Q - 1, lambda i: send(recv7.at[q], recv7.at[q], 6, s, side + lax.rem(q + Q // 2 + swing(i) + Q, Q)))
     pending.append(lambda: sent(recv7.at[pl.ds(0, Q - 1)], 6))
     loads[5].wait()
     wait_for(recv7.at[pl.ds(0, Q - 1)], recv_sem.at[6])
 
     wide = jnp.concatenate([recv7[c // per, c % per] for c in range(C)], axis=1)
     term = dot(wide, tokens[...].reshape(wide.shape[1], 128), 1, 0)
-    recv8[s] = term.astype(bf16)
+    term8[...] = term.astype(bf16)
 
     def to_plane(i):
         to = far_end(i)
 
         @pl.when(to != s)
         def _():
-            send(recv8.at[s], recv8.at[s], 7, to, x)
+            send(term8, recv8.at[s], 7, to, x)
+
+        @pl.when(to == s)
+        def _():
+            keep(term8, recv8.at[s], 7)
 
     each(S, to_plane)
 
@@ -400,27 +404,25 @@
     store_out.wait()
     store_in.wait()
     store_tok.wait()
-    wait_for(recv8.at[pl.ds(0, S - 1)], recv_sem.at[7])
-    total = recv8[0].astype(f32)
-    for i in range(1, S):
-        total = total + recv8[i].astype(f32)
-    gslot[...] = total
-    store_slot = pltpu.make_async_copy(gslot, gslot_h, out_sem.at[3])
-    store_slot.start()
-
+    wait_for(recv8, recv_sem.at[7])
     sent(recv8.at[pl.ds(0, S - 1)], 7)
-    store_slot.wait()
-
-
-def hand_over(*refs):
-    sources, targets, held, sem = refs[0:4], refs[4:8], refs[8:12], refs[12]
+
+
+def hand_over(terms_h, a_h, b_h, c_h, to_slot, to_a, to_b, to_c, terms, a, b, c, slot, sem):
+    sources, held, targets = (terms_h, a_h, b_h, c_h), (terms, a, b, c), (to_slot, to_a, to_b, to_c)
     ins = [pltpu.make_async_copy(sources[i], held[i], sem.at[i]) for i in range(4)]
-    outs = [pltpu.make_async_copy(held[i], targets[i], sem.at[4 + i]) for i in range(4)]
+    outs = [pltpu.make_async_copy((slot, a, b, c)[i], targets[i], sem.at[4 + i]) for i in range(4)]
     for copy in ins:
         copy.start()
-    for i in range(4):
+    for i in range(1, 4):
         ins[i].wait()
         outs[i].start()
+    ins[0].wait()
+    sums = [terms[i].astype(f32) for i in range(4)]
+    for i in range(4, terms.shape[0]):
+        sums[i % 4] = sums[i % 4] + terms[i].astype(f32)
+    slot[...] = (sums[0] + sums[1]) + (sums[2] + sums[3])
+    outs[0].start()
     for copy in outs:
         copy.wait()
 
@@ -441,9 +443,11 @@
         Q = E // 2
         per = C // Q
         hold = lambda a: pltpu.VMEM(a.shape, a.dtype)
+        terms = jax.ShapeDtypeStruct((S, E, D), bf16)
+        term = jax.ShapeDtypeStruct((E, D), bf16)
         scratch = (
             [hold(a) for a in args]
-            + [hold(a) for a in outs]
+            + [hold(a) for a in (outs[0], term, outs[2], outs[3])]
             + [
                 pltpu.VMEM((C, E, M), f32),
                 pltpu.VMEM((C, E, M), f32),
@@ -465,7 +469,6 @@
                 pltpu.VMEM((Q // 2, per, E, M), bf16),
                 pltpu.VMEM((Q, per, E, M), bf16),
                 pltpu.VMEM((Q, per, E, M), bf16),
-                pltpu.VMEM((S, E, D), bf16),
                 pltpu.VMEM((8, D), f32),
                 pltpu.VMEM((8, D), f32),
                 pltpu.SemaphoreType.DMA((6,)),
@@ -475,9 +478,9 @@
                 pltpu.SemaphoreType.REGULAR,
             ]
         )
-        gtok, gslot, gwin, gwout = pl.pallas_call(
+        gtok, parts, gwin, gwout = pl.pallas_call(
             functools.partial(kernel, S, E, C),
-            out_shape=outs,
+            out_shape=(outs[0], terms, outs[2], outs[3]),
             in_specs=[pl.BlockSpec(memory_space=pltpu.HBM)] * 6,
             out_specs=[pl.BlockSpec(memory_space=pl.ANY)] * 4,
             scratch_shapes=scratch,
@@ -486,14 +489,15 @@
             ),
             name="moe_backward",
         )(*args)
-        gtok, gslot, gwin, gwout = pl.pallas_call(
+        gslot, gtok, gwin, gwout = pl.pallas_call(
             hand_over,
-            out_shape=outs,
+            out_shape=(outs[1], outs[0], outs[2], outs[3]),
             in_specs=[pl.BlockSpec(memory_space=pl.ANY)] * 4,
             out_specs=[pl.BlockSpec(memory_space=pltpu.HBM)] * 4,
-            scratch_shapes=[hold(a) for a in outs] + [pltpu.SemaphoreType.DMA((8,))],
+            scratch_shapes=[hold(a) for a in (terms, outs[0], outs[2], outs[3], outs[1])]
+            + [pltpu.SemaphoreType.DMA((8,))],
             name="hand_over",
-        )(gtok, gslot, gwin, gwout)
+        )(parts, gtok, gwin, gwout)
         return gtok, gslot, gwin[None], gwout[None]
 
     in_specs = (

time: 78.1 us -> 76.9 us (0.985)
  Pallas kernels: 77.3 us -> 76.1 us
    pallas_call x2, Pallas kernels: 77.3 us -> 76.1 us  [the longest x1 73.8 us: body(): pl.pallas_call(functools.partial(kernel, S, E, C), out_shape=(outs[0], te...]
where the time goes in v6:
time: 76.9 us; the launch traced here: 76.7 us
  Pallas kernels  76.1 us (99%)
    pallas_call x1, Pallas kernels, body(): pl.pallas_call(functools.partial(kernel, S, E, C), out_shape=(outs[0], te...  73.8 us
    pallas_call x1, Pallas kernels, body(): pl.pallas_call(hand_over, out_shape=(outs[1], outs[0], outs[2], outs[3]),...  2.32 us

profile of v6, /device:TPU:1, one launch (start us, length us, event | category | flops | bytes accessed | tf_op | source)
XLA Modules:
  0.0 76.7 jit_solution(11719452133082358743)
XLA Ops:
  0.6 73.8 %moe_backward.1 = (bf16[8,256,128]{2,1,0:T(8,128)(2,1)}, bf16[32,16,128]{2,1,0:T(8,128)(2,1)}, bf16[2048,128]{1,0:T(8,128)(2,1)}, bf16[128,2048]{1,0:T(8,128)(2,1)}) custom-call(bf16[8,256,128]{2,1,0:T(8,128)(2,1)} %tokens_h.1, bf16[8,256,128]{2,1,0:T(8,128)(2,1)} %grad_h.1, f32[8,16,256]{2,1,0:T(8,128)} %logits_h.1, bf16[16,128]{1,0:T(8,128)(2,1)} %params_h.1, ...), custom_call_target="tpu_custom_call" | custom-call | tf_op jit(solution)/shard_map/moe_backward/pallas_call | solution.py:481
  74.4 2.3 %hand_over.1 = (f32[16,128]{1,0:T(8,128)}, bf16[8,256,128]{2,1,0:T(8,128)(2,1)}, bf16[2048,128]{1,0:T(8,128)(2,1)}, bf16[128,2048]{1,0:T(8,128)(2,1)}) custom-call(bf16[32,16,128]{2,1,0:T(8,128)(2,1)} %get-tuple-element.12.terms_h, bf16[8,256,128]{2,1,0:T(8,128)(2,1)} %get-tuple-element.13.a_h, bf16[2048,128]{1,0:T(8,128)(2,1)} %get-tuple-element.14.b_h, ...), custom_call_target="tpu_custom_call" | custom-call | tf_op jit(solution)/shard_map/hand_over/pallas_call | solution.py:492

commit v7 on v6

--- a/solution.py
+++ b/solution.py
@@ -335,7 +335,7 @@
     outs = jnp.swapaxes(sums[:, 0:8, :], 0, 1).astype(bf16)
     backs = jnp.swapaxes(sums[:, 8:16, :], 0, 1).astype(bf16)
     scales = rows4[...]
-    for c in range(C):
+    def logit_part(c):
         comb_grad = dot(outs[c], grad[c], 1, 1)
         disp_grad = dot(backs[c], tokens[c], 1, 1)
         dispatch = jnp.exp(logits[c] - scales[:, c : c + 1])
@@ -350,7 +350,18 @@
     core = lax.rem(x, 2)
     deep = C // 2
     pieces = Q // 2
-    send(send5.at[pl.ds((1 - core) * deep, deep)], pair, 5, s, x + 1 - 2 * core)
+
+    for parity in range(2):
+        @pl.when(core == parity)
+        def _():
+            for c in range(C):
+                if c // per % 2 != parity:
+                    logit_part(c)
+            send(send5.at[pl.ds((1 - parity) * deep, deep)], pair, 5, s, x + 1 - 2 * parity)
+            for c in range(C):
+                if c // per % 2 == parity:
+                    logit_part(c)
+
     pending.append(lambda: sent(pair, 5))
     wait_for(pair, recv_sem.at[5])
     for i in range(pieces):

time: 76.9 us -> 76.1 us (0.990)
  Pallas kernels: 76.1 us -> 74.8 us
    pallas_call x1, Pallas kernels: 73.8 us -> 72.5 us  [body(): pl.pallas_call(functools.partial(kernel, S, E, C), out_shape=(outs[0], te...]
where the time goes in v7:
time: 76.1 us; the launch traced here: 75.5 us
  Pallas kernels  74.8 us (98%)
    pallas_call x1, Pallas kernels, body(): pl.pallas_call(functools.partial(kernel, S, E, C), out_shape=(outs[0], te...  72.5 us
    pallas_call x1, Pallas kernels, body(): pl.pallas_call(hand_over, out_shape=(outs[1], outs[0], outs[2], outs[3]),...  2.32 us

profile of v7, /device:TPU:1, one launch (start us, length us, event | category | flops | bytes accessed | tf_op | source)
XLA Modules:
  0.0 75.5 jit_solution(5256908603837810365)
XLA Ops:
  0.6 72.5 %moe_backward.1 = (bf16[8,256,128]{2,1,0:T(8,128)(2,1)}, bf16[32,16,128]{2,1,0:T(8,128)(2,1)}, bf16[2048,128]{1,0:T(8,128)(2,1)}, bf16[128,2048]{1,0:T(8,128)(2,1)}) custom-call(bf16[8,256,128]{2,1,0:T(8,128)(2,1)} %tokens_h.1, bf16[8,256,128]{2,1,0:T(8,128)(2,1)} %grad_h.1, f32[8,16,256]{2,1,0:T(8,128)} %logits_h.1, bf16[16,128]{1,0:T(8,128)(2,1)} %params_h.1, ...), custom_call_target="tpu_custom_call" | custom-call | tf_op jit(solution)/shard_map/moe_backward/pallas_call | solution.py:492
  73.2 2.3 %hand_over.1 = (f32[16,128]{1,0:T(8,128)}, bf16[8,256,128]{2,1,0:T(8,128)(2,1)}, bf16[2048,128]{1,0:T(8,128)(2,1)}, bf16[128,2048]{1,0:T(8,128)(2,1)}) custom-call(bf16[32,16,128]{2,1,0:T(8,128)(2,1)} %get-tuple-element.12.terms_h, bf16[8,256,128]{2,1,0:T(8,128)(2,1)} %get-tuple-element.13.a_h, bf16[2048,128]{1,0:T(8,128)(2,1)} %get-tuple-element.14.b_h, ...), custom_call_target="tpu_custom_call" | custom-call | tf_op jit(solution)/shard_map/hand_over/pallas_call | solution.py:503

commit v8 on v7

--- a/solution.py
+++ b/solution.py
@@ -263,12 +263,6 @@
     activated, derivative = gelu_parts(pre_act[0:8])
     pre_grad = act_grad[8:16] * derivative
     stacked = jnp.concatenate([activated, pre_grad], axis=0).astype(bf16)
-    out_part = dot(stacked, wout[...], 1, 0)
-    back_part = dot(stacked, win[...], 1, 1)
-    for i in range(E):
-        cut = slice(i * 128, i * 128 + 128)
-        send3[i] = jnp.concatenate([out_part[0:8, cut], back_part[8:16, cut]], axis=0).astype(bf16)
-
     def to_home(i):
         to = jnp.where(i < Q, Q - side, side) + lax.rem(q + Q // 2 + swing(lax.rem(i, Q)) + Q, Q)
         own = jnp.logical_and(both, to == x)
@@ -281,7 +275,15 @@
         def _():
             keep(send3.at[to], recv3.at[s], 2)
 
-    each(E, to_home)
+    for turn in range(2):
+        base = side if turn else Q - side
+        cut = pl.ds(pl.multiple_of(base * 128, 128), Q * 128)
+        out_part = dot(stacked, wout[:, cut], 1, 0)
+        back_part = dot(stacked, win[cut, :], 1, 1)
+        for i in range(Q):
+            lanes = slice(i * 128, i * 128 + 128)
+            send3[base + i] = jnp.concatenate([out_part[0:8, lanes], back_part[8:16, lanes]], axis=0).astype(bf16)
+        each(Q, lambda i: to_home(i + turn * Q))
 
     def sent_parts():
         sent(send3.at[pl.ds(0, E - 1)], 2)

time: 76.1 us -> 76.6 us (level)
  Pallas kernels: 74.8 us -> 75.7 us
    pallas_call x1, Pallas kernels: 72.5 us -> 73.4 us  [body(): pl.pallas_call(functools.partial(kernel, S, E, C), out_shape=(outs[0], te...]
where the time goes in v8:
time: 76.6 us; the launch traced here: 76.4 us
  Pallas kernels  75.7 us (99%)
    pallas_call x1, Pallas kernels, body(): pl.pallas_call(functools.partial(kernel, S, E, C), out_shape=(outs[0], te...  73.4 us
    pallas_call x1, Pallas kernels, body(): pl.pallas_call(hand_over, out_shape=(outs[1], outs[0], outs[2], outs[3]),...  2.32 us

profile of v8, /device:TPU:1, one launch (start us, length us, event | category | flops | bytes accessed | tf_op | source)
XLA Modules:
  0.0 76.4 jit_solution(15180563748579404582)
XLA Ops:
  0.6 73.4 %moe_backward.1 = (bf16[8,256,128]{2,1,0:T(8,128)(2,1)}, bf16[32,16,128]{2,1,0:T(8,128)(2,1)}, bf16[2048,128]{1,0:T(8,128)(2,1)}, bf16[128,2048]{1,0:T(8,128)(2,1)}) custom-call(bf16[8,256,128]{2,1,0:T(8,128)(2,1)} %tokens_h.1, bf16[8,256,128]{2,1,0:T(8,128)(2,1)} %grad_h.1, f32[8,16,256]{2,1,0:T(8,128)} %logits_h.1, bf16[16,128]{1,0:T(8,128)(2,1)} %params_h.1, ...), custom_call_target="tpu_custom_call" | custom-call | tf_op jit(solution)/shard_map/moe_backward/pallas_call | solution.py:494
  74.1 2.3 %hand_over.1 = (f32[16,128]{1,0:T(8,128)}, bf16[8,256,128]{2,1,0:T(8,128)(2,1)}, bf16[2048,128]{1,0:T(8,128)(2,1)}, bf16[128,2048]{1,0:T(8,128)(2,1)}) custom-call(bf16[32,16,128]{2,1,0:T(8,128)(2,1)} %get-tuple-element.12.terms_h, bf16[8,256,128]{2,1,0:T(8,128)(2,1)} %get-tuple-element.13.a_h, bf16[2048,128]{1,0:T(8,128)(2,1)} %get-tuple-element.14.b_h, ...), custom_call_target="tpu_custom_call" | custom-call | tf_op jit(solution)/shard_map/hand_over/pallas_call | solution.py:505
